TPU v7x, 32 devices: a whole 2x2x4 slice. The times are simulated.
32 devices in a mesh: section: 2 (over y), dp: 16 (over z, x, core).
Axes of the slice: x: 2, y: 2, z: 4, core: 2. Of those that a mesh axis runs over, the one named last changes fastest.
Arguments:
- tokens: bfloat16 [4160, 768], P('dp'), may hold values from -6 to 6
- patch_order: int32 [64, 256], P('dp'), may hold values from 0 to 255, each once within a row
- sensor_tag: int32 [64], P('dp'), may hold values from 0 to 7
- class_token: bfloat16 [768], replicated, may hold values from -6 to 6
- sensor_table: bfloat16 [8, 768], replicated, may hold values from -3 to 3
- enc_gain_one: bfloat16 [768], replicated, may hold values from 0.25 to 1.75
- enc_qkv: bfloat16 [768, 2304], P(('section', 'dp')), may hold values from -0.21875 to 0.21875
- enc_out: bfloat16 [768, 768], P(('section', 'dp')), may hold values from -0.875 to 0.875
- enc_gain_two: bfloat16 [768], replicated, may hold values from 0.25 to 1.75
- enc_up: bfloat16 [768, 3072], P(('section', 'dp')), may hold values from -0.21875 to 0.21875
- enc_down: bfloat16 [3072, 768], P(('section', 'dp')), may hold values from -0.109375 to 0.109375
- dec_proj: bfloat16 [768, 512], P(('section', 'dp')), may hold values from -0.21875 to 0.21875
- mask_token: bfloat16 [512], replicated, may hold values from -6 to 6
- dec_gain_one: bfloat16 [512], replicated, may hold values from 0.25 to 1.75
- dec_qkv: bfloat16 [512, 1536], P(('section', 'dp')), may hold values from -0.25 to 0.25
- dec_out: bfloat16 [512, 512], P(('section', 'dp')), may hold values from -1.5 to 1.5
- dec_gain_two: bfloat16 [512], replicated, may hold values from 0.25 to 1.75
- dec_up: bfloat16 [512, 2048], P(('section', 'dp')), may hold values from -0.25 to 0.25
- dec_down: bfloat16 [2048, 512], P(('section', 'dp')), may hold values from -0.125 to 0.125
- out_grad: bfloat16 [16384, 512], P('dp'), may hold values from -6 to 6
Outputs:
- block_out: bfloat16 [16384, 512], P('dp', 'section')
- tokens_grad: float32 [4160, 768], P('dp', 'section')
- enc_qkv_grad: float32 [768, 2304], P(('section', 'dp'))
- enc_out_grad: float32 [768, 768], P(('section', 'dp'))
- enc_up_grad: float32 [768, 3072], P(('section', 'dp'))
- enc_down_grad: float32 [3072, 768], P(('section', 'dp'))
- dec_proj_grad: float32 [768, 512], P(('section', 'dp'))
- dec_qkv_grad: float32 [512, 1536], P(('section', 'dp'))
- dec_out_grad: float32 [512, 512], P(('section', 'dp'))
- dec_up_grad: float32 [512, 2048], P(('section', 'dp'))
- dec_down_grad: float32 [2048, 512], P(('section', 'dp'))
- class_token_grad: float32 [768], replicated
- sensor_table_grad: float32 [8, 768], replicated
- enc_gain_one_grad: float32 [768], replicated
- enc_gain_two_grad: float32 [768], replicated
- mask_token_grad: float32 [512], replicated
- dec_gain_one_grad: float32 [512], replicated
- dec_gain_two_grad: float32 [512], replicated
Inputs may be any that keep to these rules, and one draw needn't show every extreme that they name: `patch_order`: each row holds every patch number once; its first 64 entries are the patches of the rows 1 to 64 of that chip in tokens, in order.
All inputs are finite; a program needn't handle non-finite values.
Results may differ from a plain program's by a relative error of at most 0.018.
Values may be sent and summed in bfloat16 or wider, within the bound.
No kernel may reach another device: no remote copies, remote signals or barrier semaphores. Data moves between devices by JAX's collectives and lax.ppermute only.
A program may use at most 448 MiB of HBM per device.

v0:
```python
import math

import jax
import jax.numpy as jnp
from jax import lax
from jax.sharding import PartitionSpec as P

HEADS_E = 12
HEADS_D = 8
HEAD_DIM = 64
MICRO = 4


def shifted(block, axis, distance):
    devices = range(lax.axis_size(axis))
    route = [(i - distance, i) for i in devices if i - distance in devices]
    return lax.ppermute(block, axis, route)


def partner(value, axis, bit):
    return lax.ppermute(value, axis, [(i, i ^ 1 << bit) for i in range(lax.axis_size(axis))])


def matmul(left, right):
    return jnp.dot(left, right, preferred_element_type=jnp.float32)


def against_rows(left, right):
    return lax.dot_general(
        left, right, (((1,), (1,)), ((), ())), preferred_element_type=jnp.float32
    )


def over_rows(left, right):
    return lax.dot_general(
        left, right, (((0,), (0,)), ((), ())), preferred_element_type=jnp.float32
    )


def layer_norm(rows, gain):
    mean = jnp.mean(rows, axis=-1, keepdims=True)
    centred = rows - mean
    spread = jnp.mean(centred * centred, axis=-1, keepdims=True)
    return centred * lax.rsqrt(spread + 1e-05) * gain


def gelu_tanh(value):
    return (
        0.5
        * value
        * (1.0 + jnp.tanh(0.7978845608028654 * (value + 0.044715 * value * value * value)))
    )


def position_table(count, width):
    half = width // 2
    place = jnp.arange(count, dtype=jnp.float32)[:, None]
    rate = jnp.exp(jnp.arange(half, dtype=jnp.float32) * (-math.log(10000.0) / half))
    angle = place * rate[None, :]
    return jnp.concatenate([jnp.sin(angle), jnp.cos(angle)], axis=1)


def attend(triple, chips, heads):
    rows = triple.shape[0]
    width = triple.shape[1] // 3
    length = rows // chips
    parts = triple.reshape(chips, length, 3, heads, HEAD_DIM)
    scores = jnp.einsum(
        "cqhe,ckhe->chqk", parts[:, :, 0], parts[:, :, 1], preferred_element_type=jnp.float32
    ) * HEAD_DIM ** (-0.5)
    top = jnp.max(scores, axis=-1, keepdims=True)
    raised = jnp.exp(scores - top)
    total = jnp.sum(raised, axis=-1, keepdims=True)
    shares = (raised / total).astype(jnp.bfloat16)
    mixed = jnp.einsum(
        "chqk,ckhe->cqhe", shares, parts[:, :, 2], preferred_element_type=jnp.float32
    )
    return (mixed.astype(jnp.bfloat16).reshape(rows, width), top + jnp.log(total))


def attend_back(triple, log_total, grad_mixed, chips, heads):
    rows = triple.shape[0]
    width = triple.shape[1] // 3
    length = rows // chips
    parts = triple.reshape(chips, length, 3, heads, HEAD_DIM)
    query = parts[:, :, 0]
    key = parts[:, :, 1]
    value = parts[:, :, 2]
    scale = HEAD_DIM ** (-0.5)
    scores = jnp.einsum("cqhe,ckhe->chqk", query, key, preferred_element_type=jnp.float32) * scale
    shares = jnp.exp(scores - log_total)
    grad_heads = grad_mixed.reshape(chips, length, heads, HEAD_DIM)
    grad_value = jnp.einsum(
        "chqk,cqhe->ckhe",
        shares.astype(jnp.bfloat16),
        grad_heads,
        preferred_element_type=jnp.float32,
    )
    grad_shares = jnp.einsum(
        "cqhe,ckhe->chqk", grad_heads, value, preferred_element_type=jnp.float32
    )
    grad_scores = (
        shares * (grad_shares - jnp.sum(grad_shares * shares, axis=-1, keepdims=True))
    ).astype(jnp.bfloat16)
    grad_query = (
        jnp.einsum("chqk,ckhe->cqhe", grad_scores, key, preferred_element_type=jnp.float32) * scale
    )
    grad_key = (
        jnp.einsum("chqk,cqhe->ckhe", grad_scores, query, preferred_element_type=jnp.float32)
        * scale
    )
    grad_triple = jnp.stack([grad_query, grad_key, grad_value], axis=2)
    return grad_triple.astype(jnp.bfloat16).reshape(rows, 3 * width)


def block_forward(rows, weights, chips, heads):
    gain_one, w_triple, w_mixing, gain_two, w_expand, w_reduce = weights
    normed_one = layer_norm(rows, gain_one).astype(jnp.bfloat16)
    triple = matmul(normed_one, w_triple).astype(jnp.bfloat16)
    mixed, log_total = attend(triple, chips, heads)
    middle = rows + matmul(mixed, w_mixing)
    normed_two = layer_norm(middle, gain_two).astype(jnp.bfloat16)
    expanded = matmul(normed_two, w_expand)
    hidden = gelu_tanh(expanded).astype(jnp.bfloat16)
    result = middle + matmul(hidden, w_reduce)
    return (
        result,
        (rows, normed_one, triple, mixed, log_total, middle, normed_two, expanded, hidden),
    )


def block_back(kept, grad_out, weights, chips, heads):
    rows, normed_one, triple, mixed, log_total, middle, normed_two, expanded, hidden = kept
    gain_one, w_triple, w_mixing, gain_two, w_expand, w_reduce = weights
    grad_branch = grad_out.astype(jnp.bfloat16)
    grad_reduce = over_rows(hidden, grad_branch)
    grad_hidden = against_rows(grad_branch, w_reduce)
    _, gelu_back = jax.vjp(gelu_tanh, expanded)
    grad_expanded = gelu_back(grad_hidden)[0].astype(jnp.bfloat16)
    grad_expand = over_rows(normed_two, grad_expanded)
    grad_normed = against_rows(grad_expanded, w_expand)
    _, norm_back = jax.vjp(layer_norm, middle, gain_two)
    grad_part, grad_gain_two = norm_back(grad_normed)
    grad_middle = grad_out + grad_part
    grad_branch = grad_middle.astype(jnp.bfloat16)
    grad_mixing = over_rows(mixed, grad_branch)
    grad_mixed = against_rows(grad_branch, w_mixing).astype(jnp.bfloat16)
    grad_triple = attend_back(triple, log_total, grad_mixed, chips, heads)
    grad_weights = over_rows(normed_one, grad_triple)
    grad_normed = against_rows(grad_triple, w_triple)
    _, norm_back = jax.vjp(layer_norm, rows, gain_one)
    grad_part, grad_gain_one = norm_back(grad_normed)
    return (
        grad_middle + grad_part,
        (grad_weights, grad_mixing, grad_expand, grad_reduce),
        (grad_gain_one, grad_gain_two),
    )


def local(
    tokens,
    patch_order,
    sensor_tag,
    class_token,
    sensor_table,
    enc_gain_one,
    enc_qkv,
    enc_out,
    enc_gain_two,
    enc_up,
    enc_down,
    dec_proj,
    mask_token,
    dec_gain_one,
    dec_qkv,
    dec_out,
    dec_gain_two,
    dec_up,
    dec_down,
    out_grad,
):
    section = lax.axis_index("section")
    is_first = section == 0
    is_second = section == 1
    shards = (enc_qkv, enc_out, enc_up, enc_down, dec_proj, dec_qkv, dec_out, dec_up, dec_down)
    full = (
        lax.all_gather(enc_qkv, ("section", "dp"), axis=0, tiled=True),
        lax.all_gather(enc_out, ("section", "dp"), axis=0, tiled=True),
        lax.all_gather(enc_up, ("section", "dp"), axis=0, tiled=True),
        lax.all_gather(enc_down, ("section", "dp"), axis=0, tiled=True),
        lax.all_gather(dec_proj, ("section", "dp"), axis=0, tiled=True),
        lax.all_gather(dec_qkv, ("section", "dp"), axis=0, tiled=True),
        lax.all_gather(dec_out, ("section", "dp"), axis=0, tiled=True),
        lax.all_gather(dec_up, ("section", "dp"), axis=0, tiled=True),
        lax.all_gather(dec_down, ("section", "dp"), axis=0, tiled=True),
    )
    enc_weights = (
        enc_gain_one.astype(jnp.float32),
        full[0],
        full[1],
        enc_gain_two.astype(jnp.float32),
        full[2],
        full[3],
    )
    projection = full[4]
    dec_weights = (
        dec_gain_one.astype(jnp.float32),
        full[5],
        full[6],
        dec_gain_two.astype(jnp.float32),
        full[7],
        full[8],
    )
    chips_all = patch_order.shape[0]
    chips = chips_all // MICRO
    seq_in = tokens.shape[0] // chips_all
    seq_out = patch_order.shape[1]
    visible_count = seq_in - 1
    width_enc = tokens.shape[1]
    width_dec = out_grad.shape[1]
    sensor_count = sensor_table.shape[0]
    mlp_enc = full[2].shape[1]
    mlp_dec = full[7].shape[1]
    rows_dec = chips * seq_out
    table = position_table(seq_out, width_dec)
    places = jnp.arange(seq_out, dtype=jnp.int32)
    mask_row = mask_token.astype(jnp.float32)
    class_row = class_token.astype(jnp.float32)
    single = jnp.float32
    brain = jnp.bfloat16

    def visible_blank():
        return jnp.zeros((chips * visible_count, width_enc), brain)

    def decode_blank():
        return (
            jnp.zeros((rows_dec, width_dec), brain),
            jnp.zeros((chips * visible_count, width_enc), brain),
            (
                jnp.zeros((width_enc, width_dec), single),
                jnp.zeros((width_dec, 3 * width_dec), single),
                jnp.zeros((width_dec, width_dec), single),
                jnp.zeros((width_dec, mlp_dec), single),
                jnp.zeros((mlp_dec, width_dec), single),
            ),
            (
                jnp.zeros((width_dec,), single),
                jnp.zeros((width_dec,), single),
                jnp.zeros((width_dec,), single),
            ),
        )

    def back_blank():
        return (
            jnp.zeros((chips * seq_in, width_enc), single),
            (
                jnp.zeros((width_enc, 3 * width_enc), single),
                jnp.zeros((width_enc, width_enc), single),
                jnp.zeros((width_enc, mlp_enc), single),
                jnp.zeros((mlp_enc, width_enc), single),
            ),
            (
                jnp.zeros((width_enc,), single),
                jnp.zeros((sensor_count, width_enc), single),
                jnp.zeros((width_enc,), single),
                jnp.zeros((width_enc,), single),
            ),
        )

    def encoder_input(tok_rows, tags):
        onehot = (tags[:, None] == jnp.arange(sensor_count, dtype=jnp.int32)[None, :]).astype(
            jnp.bfloat16
        )
        sensor_rows = matmul(onehot, sensor_table)
        lead = class_row[None, None, :]
        sequence = (
            jnp.concatenate(
                [lead, tok_rows.astype(jnp.float32).reshape(chips, seq_in, width_enc)], axis=1
            )
            + sensor_rows[:, None, :]
        )
        return sequence.reshape(chips * (seq_in + 1), width_enc)

    def encode(tok_rows, tags):
        encoded, kept = block_forward(encoder_input(tok_rows, tags), enc_weights, chips, HEADS_E)
        visible = encoded.reshape(chips, seq_in + 1, width_enc)[:, 2:].reshape(
            chips * visible_count, width_enc
        )
        return (visible.astype(jnp.bfloat16), kept)

    def encode_back(kept, tags, grad_visible):
        grad_encoded = jnp.pad(
            grad_visible.astype(jnp.float32).reshape(chips, visible_count, width_enc),
            ((0, 0), (2, 0), (0, 0)),
        )
        grad_sequence, matrices, gains = block_back(
            kept, grad_encoded.reshape(-1, width_enc), enc_weights, chips, HEADS_E
        )
        grad_chip = grad_sequence.reshape(chips, seq_in + 1, width_enc)
        onehot = (tags[:, None] == jnp.arange(sensor_count, dtype=jnp.int32)[None, :]).astype(
            jnp.float32
        )
        sensor_grad = jnp.dot(onehot.T, jnp.sum(grad_chip, axis=1), precision=lax.Precision.HIGHEST)
        class_grad = jnp.sum(grad_chip[:, 0], axis=0)
        token_rows_grad = grad_chip[:, 1:].reshape(chips * seq_in, width_enc)
        return (token_rows_grad, matrices, (class_grad, sensor_grad, gains[0], gains[1]))

    def decode(pack):
        received, order, grad_rows = pack
        projected = matmul(received, projection).reshape(chips, visible_count, width_dec)
        rank = jnp.sum(
            jnp.where(order[:, :, None] == places[None, None, :], places[None, :, None], 0), axis=1
        )
        picked = jnp.take_along_axis(
            projected, jnp.minimum(rank, visible_count - 1)[:, :, None], axis=1
        )
        seen = (rank < visible_count)[:, :, None]
        decoder_in = jnp.where(seen, picked, mask_row[None, None, :]) + table[None, :, :]
        decoded, kept = block_forward(
            decoder_in.reshape(-1, width_dec), dec_weights, chips, HEADS_D
        )
        grad_in, matrices, gains = block_back(
            kept, grad_rows.astype(jnp.float32), dec_weights, chips, HEADS_D
        )
        grad_chip = grad_in.reshape(chips, seq_out, width_dec)
        mask_grad = jnp.sum(jnp.where(seen, 0.0, grad_chip), axis=(0, 1))
        grad_projected = jnp.take_along_axis(grad_chip, order[:, :visible_count, None], axis=1)
        grad_projected = grad_projected.reshape(chips * visible_count, width_dec).astype(
            jnp.bfloat16
        )
        proj_grad = over_rows(received, grad_projected)
        grad_visible = against_rows(grad_projected, projection).astype(jnp.bfloat16)
        return (
            decoded.astype(jnp.bfloat16),
            grad_visible,
            (proj_grad,) + matrices,
            (mask_grad, gains[0], gains[1]),
        )

    def decode_spare(pack):
        return decode_blank()

    big_total = tuple((jnp.zeros(matrix.shape, jnp.float32) for matrix in full))
    big_shard = tuple((jnp.zeros(piece.shape, jnp.float32) for piece in shards))
    small_total = (
        jnp.zeros((width_enc,), jnp.float32),
        jnp.zeros((sensor_count, width_enc), jnp.float32),
        jnp.zeros((width_enc,), jnp.float32),
        jnp.zeros((width_enc,), jnp.float32),
        jnp.zeros((width_dec,), jnp.float32),
        jnp.zeros((width_dec,), jnp.float32),
        jnp.zeros((width_dec,), jnp.float32),
    )
    out_parts = []
    grad_parts = []
    for step in range(MICRO):
        tok_rows = tokens[step * chips * seq_in : (step + 1) * chips * seq_in]
        tags = sensor_tag[step * chips : (step + 1) * chips]
        order = patch_order[step * chips : (step + 1) * chips]
        grad_rows = out_grad[step * chips * seq_out : (step + 1) * chips * seq_out]

        def first_pass(pack):
            return encode(pack[0], pack[1])[0]

        def first_spare(pack):
            return visible_blank()

        visible = lax.cond(is_first, first_pass, first_spare, (tok_rows, tags))
        received = shifted(visible, "section", 1)
        decoded, grad_visible, dec_big, dec_small = lax.cond(
            is_second, decode, decode_spare, (received, order, grad_rows)
        )
        grad_received = shifted(grad_visible, "section", -1)

        def back_grads(pack):
            kept_again = encode(pack[0], pack[1])[1]
            return encode_back(kept_again, pack[1], pack[2])

        def back_spare(pack):
            return back_blank()

        token_part, enc_big, enc_small = lax.cond(
            is_first, back_grads, back_spare, (tok_rows, tags, grad_received)
        )
        step_big = enc_big + dec_big
        big_total = tuple((total + piece for total, piece in zip(big_total, step_big)))
        small_total = tuple(
            (total + piece for total, piece in zip(small_total, enc_small + dec_small))
        )
        out_parts.append(decoded)
        grad_parts.append(token_part)
    big_shard = lax.psum_scatter(big_total, ("section", "dp"), scatter_dimension=0, tiled=True)
    small = lax.psum(small_total, ("section", "dp"))
    block_rows = jnp.concatenate(out_parts, axis=0)
    token_rows = jnp.concatenate(grad_parts, axis=0)
    half_enc = width_enc // 2
    half_dec = width_dec // 2
    came = (
        partner(token_rows[:, half_enc:].astype(jnp.bfloat16), "section", 0).astype(jnp.float32),
        partner(
            block_rows[:, :half_dec].astype(jnp.float32).astype(jnp.bfloat16), "section", 0
        ).astype(jnp.float32),
    )
    token_share = jnp.where(is_first, token_rows[:, :half_enc], came[0])
    block_share = jnp.where(is_first, came[1], block_rows[:, half_dec:].astype(jnp.float32)).astype(
        jnp.bfloat16
    )
    return (block_share, token_share) + tuple(big_shard) + tuple(small)


def solution(mesh):
    in_specs = (
        P("dp", None),
        P("dp", None),
        P("dp"),
        P(),
        P(),
        P(),
        P(("section", "dp"), None),
        P(("section", "dp"), None),
        P(),
        P(("section", "dp"), None),
        P(("section", "dp"), None),
        P(("section", "dp"), None),
        P(),
        P(),
        P(("section", "dp"), None),
        P(("section", "dp"), None),
        P(),
        P(("section", "dp"), None),
        P(("section", "dp"), None),
        P("dp", None),
    )
    out_specs = (
        P("dp", "section"),
        P("dp", "section"),
        P(("section", "dp"), None),
        P(("section", "dp"), None),
        P(("section", "dp"), None),
        P(("section", "dp"), None),
        P(("section", "dp"), None),
        P(("section", "dp"), None),
        P(("section", "dp"), None),
        P(("section", "dp"), None),
        P(("section", "dp"), None),
        P(),
        P(),
        P(),
        P(),
        P(),
        P(),
        P(),
    )
    return jax.shard_map(local, mesh=mesh, in_specs=in_specs, out_specs=out_specs, check_vma=False)
```

profile of v0, /device:TPU:0, one launch (start us, length us, event | category | flops | bytes accessed | tf_op | source)
XLA Modules:
  0.0 1764.5 jit_solution(3050193798295102406)
XLA Ops:
  21.1 44.9 %all_gather.33 = bf16[512,512]{1,0:T(8,128)(2,1)S(1)} all-gather(bf16[16,512]{1,0:T(8,128)(2,1)S(1)} %copy-done.248), channel_id=1, replica_groups=mesh['section'=2,'dp'=16] {'section','dp'}, dimensions={0}, use_global_device_ids=true | all-gather | bytes 540672 | tf_op jit(solution)/shard_map/all_gather | solution.py:193
  66.0 39.6 %all_gather.31 = bf16[768,512]{1,0:T(8,128)(2,1)S(1)} all-gather(bf16[24,512]{1,0:T(8,128)(2,1)S(1)} %copy-done.231), channel_id=1, replica_groups=mesh['section'=2,'dp'=16] {'section','dp'}, dimensions={0}, use_global_device_ids=true | all-gather | bytes 811008 | tf_op jit(solution)/shard_map/all_gather | solution.py:191
  105.6 25.2 %all-gather.8.cloned.1.call-done = bf16[768,2304]{1,0:T(8,128)(2,1)} async-done(((bf16[24,2304]{1,0:T(8,128)(2,1)}), bf16[768,2304]{1,0:T(8,128)(2,1)}) %all-gather.8.cloned.1.call-update) | async-done | bytes 3538960 | tf_op jit(solution)/shard_map/all_gather | solution.py:187
  130.8 65.3 %all-gather.12.cloned.1.call-done = bf16[768,3072]{1,0:T(8,128)(2,1)} async-done(((bf16[24,3072]{1,0:T(8,128)(2,1)}), bf16[768,3072]{1,0:T(8,128)(2,1)}) %all-gather.12.cloned.1.call-update) | async-done | bytes 4718608 | tf_op jit(solution)/shard_map/all_gather | solution.py:189
  196.1 65.2 %all-gather.14.cloned.1.call-done = bf16[3072,768]{1,0:T(8,128)(2,1)} async-done(((bf16[96,768]{1,0:T(8,128)(2,1)}), bf16[3072,768]{1,0:T(8,128)(2,1)}) %all-gather.14.cloned.1.call-update) | async-done | bytes 4718608 | tf_op jit(solution)/shard_map/all_gather | solution.py:190
  261.3 16.7 conditional.18
  271.6 5.7 fusion.118
  279.9 16.8 conditional.14
  290.3 5.7 fusion.42
  298.6 15.4 conditional.12
  308.3 5.7 fusion.4
  316.0 16.7 conditional.16
  326.3 5.7 fusion.80
  336.5 39.5 %all-gather.18.cloned.1.call-done = bf16[512,2048]{1,0:T(8,128)(2,1)} async-done(((bf16[16,2048]{1,0:T(8,128)(2,1)}), bf16[512,2048]{1,0:T(8,128)(2,1)}) %all-gather.18.cloned.1.call-update) | async-done | bytes 2097168 | tf_op jit(solution)/shard_map/all_gather | solution.py:194
  376.0 58.2 %all-gather.20.cloned.1.call-done = bf16[2048,512]{1,0:T(8,128)(2,1)} async-done(((bf16[64,512]{1,0:T(8,128)(2,1)}), bf16[2048,512]{1,0:T(8,128)(2,1)}) %all-gather.20.cloned.1.call-update) | async-done | bytes 2097168 | tf_op jit(solution)/shard_map/all_gather | solution.py:195
  434.2 5.0 conditional.13
  443.5 10.1 conditional.15
  457.9 9.8 conditional.17
  471.9 13.3 conditional.19
  485.2 4.3 add_add_fusion.39
  489.6 3.8 add_add_fusion.40
  498.7 140.3 %collective-permute-done.8 = bf16[64,768]{1,0:T(8,128)(2,1)S(1)} collective-permute-done((bf16[64,768]{1,0:T(8,128)(2,1)}, bf16[64,768]{1,0:T(8,128)(2,1)S(1)}, u32[]{:S(2)}, u32[]{:S(2)}) %collective-permute-start.8) | collective-permute-done | bytes 98336 | tf_op jit(solution)/shard_map/ppermute | solution.py:17
  639.0 39.7 %conditional.23 = (f32[65,768]{1,0:T(8,128)}, f32[768,2304]{1,0:T(8,128)S(1)}, f32[768,768]{1,0:T(8,128)}, f32[768,3072]{1,0:T(8,128)S(1)}, f32[3072,768]{1,0:T(...) conditional(s32[]{:T(128)} %convert_element_type.771, () %tuple.120, ...), branch_computations={%region_148.151_spmd, %region_149.166_spmd} | conditional | flops 2544070656 | bytes 131535408 | solution.py:382
  684.5 3.0 copy-done.18
  687.6 55.0 %conditional.22 = (f32[65,768]{1,0:T(8,128)}, f32[768,2304]{1,0:T(8,128)}, f32[768,768]{1,0:T(8,128)S(1)}, f32[768,3072]{1,0:T(8,128)S(1)}, f32[3072,768]{1,0:T(...) conditional(s32[]{:T(128)} %convert_element_type.771, () %tuple.118, ...), branch_computations={%region_132.135_spmd, %region_133.150_spmd} | conditional | flops 2544070656 | bytes 130355680 | solution.py:382
  734.1 4.1 fusion.296
  742.7 3.5 copy-done.19
  749.8 45.3 %conditional.21 = (f32[65,768]{1,0:T(8,128)}, f32[768,2304]{1,0:T(8,128)}, f32[768,768]{1,0:T(8,128)S(1)}, f32[768,3072]{1,0:T(8,128)S(1)}, f32[3072,768]{1,0:T(...) conditional(s32[]{:T(128)} %convert_element_type.771, () %tuple.116, ...), branch_computations={%region_116.119_spmd, %region_117.134_spmd} | conditional | flops 2544070656 | bytes 130355680 | solution.py:382
  786.9 4.1 fusion.246
  795.1 3.5 copy-done.21
  802.3 50.3 %conditional.20 = (f32[65,768]{1,0:T(8,128)S(1)}, f32[768,2304]{1,0:T(8,128)}, f32[768,768]{1,0:T(8,128)S(1)}, f32[768,3072]{1,0:T(8,128)}, f32[3072,768]{1,0:T(...) conditional(s32[]{:T(128)} %convert_element_type.771, ...), branch_computations={%region_100.103_spmd, %region_101.118_spmd} | conditional | flops 2544070656 | bytes 130343360 | solution.py:382
  837.0 4.1 fusion.196
  841.2 6.1 fusion.163
  847.3 5.1 fusion.197
  853.3 5.3 add_add_fusion.38
  858.7 6.9 add_add_fusion.37
  865.7 10.2 add_add_fusion.36
  876.0 10.1 add_add_fusion.35
  886.2 13.5 add_add_fusion.34
  899.8 17.5 add_add_fusion.33
  917.3 17.0 add_add_fusion.32
  944.0 45.5 %all-reduce.4 = (f32[768]{0:T(1024)}, f32[8,768]{1,0:T(8,128)}, f32[768]{0:T(1024)}, f32[768]{0:T(1024)}, f32[512]{0:T(512)}, /*index=5*/f32[512]{0:T(512)}, f32[512]{0:T(512)}) all-reduce(f32[768]{0:T(1024)S(1)} %add_add_fusion.44, f32[8,768]{1,0:T(8,128)S(1)} %add_add_fusion.41, ...), channel_id=1, replica_groups=mesh['section'=2,'dp'=16] {'section','dp'}, use_global_device_ids=true, to_apply=%region_173.176 | all-reduce | flops 9984 | bytes 79872 | tf_op jit(solution)/shard_map/psum | solution.py:393
  991.2 78.5 %reduce-scatter.20.cloned.1.call-done = f32[16,1536]{1,0:T(8,128)} async-done(((f32[512,1536]{1,0:T(8,128)}), f32[16,1536]{1,0:T(8,128)}) %reduce-scatter.20.cloned.1.call-update) | async-done | bytes 98320 | tf_op jit(solution)/shard_map/reduce_scatter | solution.py:392
  1069.7 142.8 %reduce-scatter.24.cloned.1.call-done = f32[16,2048]{1,0:T(8,128)} async-done(((f32[512,2048]{1,0:T(8,128)}), f32[16,2048]{1,0:T(8,128)}) %reduce-scatter.24.cloned.1.call-update) | async-done | bytes 131088 | tf_op jit(solution)/shard_map/reduce_scatter | solution.py:392
  1212.5 140.5 %reduce-scatter.26.cloned.1.call-done = f32[64,512]{1,0:T(8,128)} async-done(((f32[2048,512]{1,0:T(8,128)}), f32[64,512]{1,0:T(8,128)}) %reduce-scatter.26.cloned.1.call-update) | async-done | bytes 131088 | tf_op jit(solution)/shard_map/reduce_scatter | solution.py:392
  1353.0 121.8 %reduce-scatter.10.cloned.1.call-done = f32[24,2304]{1,0:T(8,128)} async-done(((f32[768,2304]{1,0:T(8,128)}), f32[24,2304]{1,0:T(8,128)}) %reduce-scatter.10.cloned.1.call-update) | async-done | bytes 221200 | tf_op jit(solution)/shard_map/reduce_scatter | solution.py:392
  1474.8 142.1 %reduce-scatter.14.cloned.1.call-done = f32[24,3072]{1,0:T(8,128)} async-done(((f32[768,3072]{1,0:T(8,128)}), f32[24,3072]{1,0:T(8,128)}) %reduce-scatter.14.cloned.1.call-update) | async-done | bytes 294928 | tf_op jit(solution)/shard_map/reduce_scatter | solution.py:392
  1616.9 140.8 %reduce-scatter.16.cloned.1.call-done = f32[96,768]{1,0:T(8,128)} async-done(((f32[3072,768]{1,0:T(8,128)}), f32[96,768]{1,0:T(8,128)}) %reduce-scatter.16.cloned.1.call-update) | async-done | bytes 294928 | tf_op jit(solution)/shard_map/reduce_scatter | solution.py:392
  (801 shorter events, 287.0 us)
Async XLA Ops:
  7.2 13.9 copy-start.248
  7.2 58.8 %copy-start.231 = (bf16[24,512]{1,0:T(8,128)(2,1)S(1)}, bf16[24,512]{1,0:T(8,128)(2,1)}, u32[]{:S(2)}) copy-start(bf16[24,512]{1,0:T(8,128)(2,1)} %param.59) | copy-start | bytes 73732
  7.2 254.1 %copy-start.204 = (bf16[8,768]{1,0:T(8,128)(2,1)S(1)}, bf16[8,768]{1,0:T(8,128)(2,1)}, u32[]{:S(2)}) copy-start(bf16[8,768]{1,0:T(8,128)(2,1)} %param.52) | copy-start | bytes 36868
  7.2 98.4 %all-gather.10.cloned.1.call-start = ((), (), s32[]{:S(2)}) async-start(), calls=%async_computation.10 | async-start | bytes 1216512 | tf_op jit(solution)/shard_map/all_gather | solution.py:188
  8.0 122.9 %all-gather.8.cloned.1.call-start = ((), (), s32[]{:S(2)}) async-start(), calls=%async_computation.9 | async-start | bytes 3649536 | tf_op jit(solution)/shard_map/all_gather | solution.py:187
  8.7 187.4 %all-gather.12.cloned.1.call-start = ((), (), s32[]{:S(2)}) async-start(), calls=%async_computation.11 | async-start | bytes 4866048 | tf_op jit(solution)/shard_map/all_gather | solution.py:189
  9.4 251.8 %all-gather.14.cloned.1.call-start = ((), (), s32[]{:S(2)}) async-start(), calls=%async_computation.12 | async-start | bytes 4866048 | tf_op jit(solution)/shard_map/all_gather | solution.py:190
  10.0 326.5 %all-gather.16.cloned.1.call-start = ((), (), s32[]{:S(2)}) async-start(), calls=%async_computation.13 | async-start | bytes 1622016 | tf_op jit(solution)/shard_map/all_gather | solution.py:192
  10.6 365.4 %all-gather.18.cloned.1.call-start = ((), (), s32[]{:S(2)}) async-start(), calls=%async_computation.14 | async-start | bytes 2162688 | tf_op jit(solution)/shard_map/all_gather | solution.py:194
  11.2 423.0 %all-gather.20.cloned.1.call-start = ((), (), s32[]{:S(2)}) async-start(), calls=%async_computation.15 | async-start | bytes 2162688 | tf_op jit(solution)/shard_map/all_gather | solution.py:195
  11.9 979.2 %reduce-scatter.18.cloned.1.call-start = ((), (), s32[]{:S(2)}) async-start(), calls=%async_computation.20 | async-start | bytes 1622016 | tf_op jit(solution)/shard_map/reduce_scatter | solution.py:392
  14.7 301.2 %copy-start.206 = (f32[768]{0:T(1024)}, f32[768]{0:T(1024)S(1)}, u32[]{:S(2)}) copy-start(f32[768]{0:T(1024)S(1)} %convert_element_type.772) | copy-start | bytes 9220
  15.4 300.6 %copy-start.134 = (f32[768]{0:T(1024)}, f32[768]{0:T(1024)S(1)}, u32[]{:S(2)}) copy-start(f32[768]{0:T(1024)S(1)} %convert_element_type.773) | copy-start | bytes 9220
  16.1 299.9 %copy-start.132 = (f32[768]{0:T(1024)}, f32[768]{0:T(1024)S(1)}, u32[]{:S(2)}) copy-start(f32[768]{0:T(1024)S(1)} %convert_element_type.774) | copy-start | bytes 9220
  21.1 277.6 %copy-start.192 = (bf16[65,768]{1,0:T(8,128)(2,1)}, bf16[65,768]{1,0:T(8,128)(2,1)S(1)}, u32[]{:S(2)}) copy-start(bf16[65,768]{1,0:T(8,128)(2,1)S(1)} %get-tuple-element.789) | copy-start | bytes 299524
  278.0 189.7 %collective-permute-start.3 = (bf16[64,768]{1,0:T(8,128)(2,1)}, bf16[64,768]{1,0:T(8,128)(2,1)}, u32[]{:S(2)}, u32[]{:S(2)}) collective-permute-start(bf16[64,768]{1,0:T(8,128)(2,1)} %get-tuple-element.964), channel_id=1, source_target_pairs={{0,16},{1,17},{2,18},{3,19},{4,20},{5,21},{6,22},{7,23},{8,24},{9,... | collective-permute-start | bytes 294920 | tf_op jit(solution)/shard_map/ppermute | solution.py:17
  296.7 142.6 %collective-permute-start.1 = (bf16[64,768]{1,0:T(8,128)(2,1)}, bf16[64,768]{1,0:T(8,128)(2,1)}, u32[]{:S(2)}, u32[]{:S(2)}) collective-permute-start(bf16[64,768]{1,0:T(8,128)(2,1)} %get-tuple-element.962), channel_id=1, source_target_pairs={{0,16},{1,17},{2,18},{3,19},{4,20},{5,21},{6,22},{7,23},{8,24},{9,... | collective-permute-start | bytes 294920 | tf_op jit(solution)/shard_map/ppermute | solution.py:17
  314.6 119.5 %collective-permute-start = (bf16[64,768]{1,0:T(8,128)(2,1)}, bf16[64,768]{1,0:T(8,128)(2,1)S(1)}, u32[]{:S(2)}, u32[]{:S(2)}) collective-permute-start(bf16[64,768]{1,0:T(8,128)(2,1)} %copy-done.227), channel_id=1, source_target_pairs={{0,16},{1,17},{2,18},{3,19},{4,20},{5,21},{6,22},{7,23},{8,24},{9,... | collective-permute-start | bytes 294920 | tf_op jit(solution)/shard_map/ppermute | solution.py:17
  315.9 118.2 %copy-start.302 = (s32[4,256]{1,0:T(4,128)S(1)}, s32[4,256]{1,0:T(4,128)}, u32[]{:S(2)}) copy-start(s32[4,256]{1,0:T(4,128)} %param.49) | copy-start | bytes 12292
  332.7 121.0 %collective-permute-start.2 = (bf16[64,768]{1,0:T(8,128)(2,1)}, bf16[64,768]{1,0:T(8,128)(2,1)}, u32[]{:S(2)}, u32[]{:S(2)}) collective-permute-start(bf16[64,768]{1,0:T(8,128)(2,1)} %get-tuple-element.963), channel_id=1, source_target_pairs={{0,16},{1,17},{2,18},{3,19},{4,20},{5,21},{6,22},{7,23},{8,24},{9,... | collective-permute-start | bytes 294920 | tf_op jit(solution)/shard_map/ppermute | solution.py:17
  489.5 501.6 %reduce-scatter.22.cloned.1.call-start = ((), (), s32[]{:S(2)}) async-start(), calls=%async_computation.22 | async-start | bytes 1081344 | tf_op jit(solution)/shard_map/reduce_scatter | solution.py:392
  489.6 149.4 %copy-start.4 = (bf16[768,2304]{1,0:T(8,128)(2,1)S(1)}, bf16[768,2304]{1,0:T(8,128)(2,1)}, u32[]{:S(2)}) copy-start(bf16[768,2304]{1,0:T(8,128)(2,1)} %all-gather.8.cloned.1.call-done) | copy-start | bytes 10616836
  489.6 149.4 %copy-start.133 = (f32[768]{0:T(1024)S(1)}, f32[768]{0:T(1024)}, u32[]{:S(2)}) copy-start(f32[768]{0:T(1024)} %copy-done.132) | copy-start | bytes 9220
  489.6 149.4 %copy-start.135 = (f32[768]{0:T(1024)S(1)}, f32[768]{0:T(1024)}, u32[]{:S(2)}) copy-start(f32[768]{0:T(1024)} %copy-done.134) | copy-start | bytes 9220
  489.6 149.4 %copy-start.207 = (f32[768]{0:T(1024)S(1)}, f32[768]{0:T(1024)}, u32[]{:S(2)}) copy-start(f32[768]{0:T(1024)} %copy-done.206) | copy-start | bytes 9220
  493.5 497.7 %reduce-scatter.12.cloned.1.call-start = ((), (), s32[]{:S(2)}) async-start(), calls=%async_computation.17 | async-start | bytes 2433024 | tf_op jit(solution)/shard_map/reduce_scatter | solution.py:392
  493.5 145.5 %collective-permute-start.8 = (bf16[64,768]{1,0:T(8,128)(2,1)}, bf16[64,768]{1,0:T(8,128)(2,1)S(1)}, u32[]{:S(2)}, u32[]{:S(2)}) collective-permute-start(bf16[64,768]{1,0:T(8,128)(2,1)} %get-tuple-element.542), channel_id=1, source_target_pairs={{16,0},{17,1},{18,2},{19,3},{20,4},{21,5},{22,6},{23,7},{24,8},{25... | collective-permute-start | bytes 294920 | tf_op jit(solution)/shard_map/ppermute | solution.py:17
  494.8 183.9 %collective-permute-start.7 = (bf16[64,768]{1,0:T(8,128)(2,1)}, bf16[64,768]{1,0:T(8,128)(2,1)}, u32[]{:S(2)}, u32[]{:S(2)}) collective-permute-start(bf16[64,768]{1,0:T(8,128)(2,1)} %copy-done.226), channel_id=1, source_target_pairs={{16,0},{17,1},{18,2},{19,3},{20,4},{21,5},{22,6},{23,7},{24,8},{25... | collective-permute-start | bytes 294920 | tf_op jit(solution)/shard_map/ppermute | solution.py:17
  496.1 246.5 %collective-permute-start.6 = (bf16[64,768]{1,0:T(8,128)(2,1)}, bf16[64,768]{1,0:T(8,128)(2,1)}, u32[]{:S(2)}, u32[]{:S(2)}) collective-permute-start(bf16[64,768]{1,0:T(8,128)(2,1)} %get-tuple-element.538), channel_id=1, source_target_pairs={{16,0},{17,1},{18,2},{19,3},{20,4},{21,5},{22,6},{23,7},{24,8},{25... | collective-permute-start | bytes 294920 | tf_op jit(solution)/shard_map/ppermute | solution.py:17
  497.4 297.7 %collective-permute-start.5 = (bf16[64,768]{1,0:T(8,128)(2,1)}, bf16[64,768]{1,0:T(8,128)(2,1)}, u32[]{:S(2)}, u32[]{:S(2)}) collective-permute-start(bf16[64,768]{1,0:T(8,128)(2,1)} %copy-done.224), channel_id=1, source_target_pairs={{16,0},{17,1},{18,2},{19,3},{20,4},{21,5},{22,6},{23,7},{24,8},{25... | collective-permute-start | bytes 294920 | tf_op jit(solution)/shard_map/ppermute | solution.py:17
  678.8 8.8 copy-start.18
  711.0 7.5 copy-start.105
  711.0 7.5 copy-start.234
  711.2 7.3 copy-start.256
  763.6 7.5 copy-start.107
  763.6 7.5 copy-start.236
  763.9 7.3 copy-start.258
  816.2 7.5 copy-start.109
  816.3 7.5 copy-start.238
  816.5 7.3 copy-start.260
  858.6 211.0 %reduce-scatter.20.cloned.1.call-start = ((), (), s32[]{:S(2)}) async-start(), calls=%async_computation.21 | async-start | bytes 3244032 | tf_op jit(solution)/shard_map/reduce_scatter | solution.py:392
  865.6 346.9 %reduce-scatter.24.cloned.1.call-start = ((), (), s32[]{:S(2)}) async-start(), calls=%async_computation.23 | async-start | bytes 4325376 | tf_op jit(solution)/shard_map/reduce_scatter | solution.py:392
  875.9 477.1 %reduce-scatter.26.cloned.1.call-start = ((), (), s32[]{:S(2)}) async-start(), calls=%async_computation.24 | async-start | bytes 4325376 | tf_op jit(solution)/shard_map/reduce_scatter | solution.py:392
  886.2 588.7 %reduce-scatter.10.cloned.1.call-start = ((), (), s32[]{:S(2)}) async-start(), calls=%async_computation.16 | async-start | bytes 7299072 | tf_op jit(solution)/shard_map/reduce_scatter | solution.py:392
  899.7 717.2 %reduce-scatter.14.cloned.1.call-start = ((), (), s32[]{:S(2)}) async-start(), calls=%async_computation.18 | async-start | bytes 9732096 | tf_op jit(solution)/shard_map/reduce_scatter | solution.py:392
  917.2 840.5 %reduce-scatter.16.cloned.1.call-start = ((), (), s32[]{:S(2)}) async-start(), calls=%async_computation.19 | async-start | bytes 9732096 | tf_op jit(solution)/shard_map/reduce_scatter | solution.py:392
  938.3 52.0 %collective-permute-start.4 = (bf16[1024,256]{1,0:T(8,128)(2,1)S(1)}, bf16[1024,256]{1,0:T(8,128)(2,1)S(1)}, u32[]{:S(2)}, u32[]{:S(2)}) collective-permute-start(bf16[1024,256]{1,0:T(8,128)(2,1)S(1)} %slice.341), channel_id=1, source_target_pairs={{0,16},{16,0},{1,17},{17,1},{2,18},{18,2},{3,19},{19,3},{4,20},{20... | collective-permute-start | bytes 1572872 | tf_op jit(solution)/shard_map/ppermute | solution.py:21
  939.7 49.8 %collective-permute-start.9 = (bf16[260,384]{1,0:T(8,128)(2,1)S(1)}, bf16[260,384]{1,0:T(8,128)(2,1)S(1)}, u32[]{:S(2)}, u32[]{:S(2)}) collective-permute-start(bf16[260,384]{1,0:T(8,128)(2,1)S(1)} %slice.524), channel_id=1, source_target_pairs={{0,16},{16,0},{1,17},{17,1},{2,18},{18,2},{3,19},{19,3},{4,20},{20... | collective-permute-start | bytes 599048 | tf_op jit(solution)/shard_map/ppermute | solution.py:21
  (198 other events, 603.6 us)
Sparse Core Ops, SparseCore 0:
  10.9 56.9 all-gather.9
  70.8 59.9 all-gather.7
  133.7 62.3 all-gather.11
  198.9 62.3 all-gather.13
  264.0 53.8 all-gather.15
  320.6 55.3 all-gather.17
  378.8 55.2 all-gather.19
  489.6 234.7 reduce-scatter.17
  727.3 133.7 reduce-scatter.21
  867.7 95.4 reduce-scatter.11
  969.2 100.4 reduce-scatter.19
  1072.4 140.0 reduce-scatter.23
  1215.3 137.6 reduce-scatter.25
  1359.1 115.6 reduce-scatter.9
  1482.1 134.7 reduce-scatter.13
  1623.2 134.4 reduce-scatter.15
where the time goes:
time: 1770 us; the launch traced here: 1760 us
  waiting for transfers between devices  1160 us (66%)
  matrix products  179 us (10%)
  blocking collectives  130 us (7%)
  other arithmetic  128 us (7%)
  local copies, waits for them, and re-layouts  106 us (6%)
  loops' own time  27.2 us (2%)
    reduce_scatter x9, waiting for transfers between devices, local(): lax.psum_scatter(big_total, ('section', 'dp'), scatter_dimension=0, tiled...  767 us
    ppermute x8, waiting for transfers between devices, shifted(): return lax.ppermute(block, axis, route)  140 us
    add x14, other arithmetic, local(): total + piece  90.9 us
    dot_general x32, matrix products, matmul(): return jnp.dot(left, right, preferred_element_type=jnp.float32)  65.7 us
    all_gather x1, waiting for transfers between devices, local(): lax.all_gather(enc_up, ('section', 'dp'), axis=0, tiled=True)  65.3 us
    all_gather x1, waiting for transfers between devices, local(): lax.all_gather(enc_down, ('section', 'dp'), axis=0, tiled=True)  65.2 us
    all_gather x1, waiting for transfers between devices, local(): lax.all_gather(dec_down, ('section', 'dp'), axis=0, tiled=True)  58.2 us
    psum x1, blocking collectives, local(): small = lax.psum(small_total, ('section', 'dp'))  45.5 us
  transfers between devices with their start and end apart: 26, of which 12 were waited for; matrix products, arithmetic and copies ran while one was open for 20% of the time, Pallas kernels for 0%

commit v1 on v0

v1 whole, which is shorter than its diff:
```python
import math

import jax
import jax.numpy as jnp
from jax import lax
from jax.sharding import PartitionSpec as P

HEADS_E = 12
HEADS_D = 8
HEAD_DIM = 64
BF = jnp.bfloat16
F32 = jnp.float32


def matmul(left, right):
    return jnp.dot(left, right, preferred_element_type=F32)


def against_rows(left, right):
    return lax.dot_general(left, right, (((1,), (1,)), ((), ())), preferred_element_type=F32)


def over_rows(left, right):
    return lax.dot_general(left, right, (((0,), (0,)), ((), ())), preferred_element_type=F32)


def layer_norm(rows, gain):
    mean = jnp.mean(rows, axis=-1, keepdims=True)
    centred = rows - mean
    spread = jnp.mean(centred * centred, axis=-1, keepdims=True)
    return centred * lax.rsqrt(spread + 1e-05) * gain


def gelu_tanh(value):
    return (
        0.5
        * value
        * (1.0 + jnp.tanh(0.7978845608028654 * (value + 0.044715 * value * value * value)))
    )


def position_table(count, width):
    half = width // 2
    place = jnp.arange(count, dtype=F32)[:, None]
    rate = jnp.exp(jnp.arange(half, dtype=F32) * (-math.log(10000.0) / half))
    angle = place * rate[None, :]
    return jnp.concatenate([jnp.sin(angle), jnp.cos(angle)], axis=1)


def attend(triple, chips, heads):
    rows = triple.shape[0]
    width = triple.shape[1] // 3
    length = rows // chips
    parts = triple.reshape(chips, length, 3, heads, HEAD_DIM)
    scores = jnp.einsum(
        "cqhe,ckhe->chqk", parts[:, :, 0], parts[:, :, 1], preferred_element_type=F32
    ) * HEAD_DIM ** (-0.5)
    top = jnp.max(scores, axis=-1, keepdims=True)
    raised = jnp.exp(scores - top)
    exact = raised / jnp.sum(raised, axis=-1, keepdims=True)
    shares = exact.astype(BF)
    mixed = jnp.einsum("chqk,ckhe->cqhe", shares, parts[:, :, 2], preferred_element_type=F32)
    return mixed.astype(BF).reshape(rows, width), exact


def attend_back(triple, exact, grad_mixed, chips, heads):
    rows = triple.shape[0]
    width = triple.shape[1] // 3
    length = rows // chips
    parts = triple.reshape(chips, length, 3, heads, HEAD_DIM)
    query, key, value = parts[:, :, 0], parts[:, :, 1], parts[:, :, 2]
    scale = HEAD_DIM ** (-0.5)
    grad_heads = grad_mixed.reshape(chips, length, heads, HEAD_DIM)
    grad_value = jnp.einsum(
        "chqk,cqhe->ckhe", exact.astype(BF), grad_heads, preferred_element_type=F32
    )
    grad_shares = jnp.einsum("cqhe,ckhe->chqk", grad_heads, value, preferred_element_type=F32)
    grad_scores = (
        exact * (grad_shares - jnp.sum(grad_shares * exact, axis=-1, keepdims=True))
    ).astype(BF)
    grad_query = (
        jnp.einsum("chqk,ckhe->cqhe", grad_scores, key, preferred_element_type=F32) * scale
    )
    grad_key = (
        jnp.einsum("chqk,cqhe->ckhe", grad_scores, query, preferred_element_type=F32) * scale
    )
    grad_triple = jnp.stack([grad_query, grad_key, grad_value], axis=2)
    return grad_triple.astype(BF).reshape(rows, 3 * width)


def block_forward(rows, weights, chips, heads):
    gain_one, w_triple, w_mixing, gain_two, w_expand, w_reduce = weights
    normed_one = layer_norm(rows, gain_one).astype(BF)
    triple = matmul(normed_one, w_triple).astype(BF)
    mixed, exact = attend(triple, chips, heads)
    middle = rows + matmul(mixed, w_mixing)
    normed_two = layer_norm(middle, gain_two).astype(BF)
    expanded = matmul(normed_two, w_expand)
    hidden = gelu_tanh(expanded).astype(BF)
    result = middle + matmul(hidden, w_reduce)
    return result, (rows, normed_one, triple, mixed, exact, middle, normed_two, expanded, hidden)


def block_back(kept, grad_out, weights, chips, heads):
    rows, normed_one, triple, mixed, exact, middle, normed_two, expanded, hidden = kept
    gain_one, w_triple, w_mixing, gain_two, w_expand, w_reduce = weights
    grad_branch = grad_out.astype(BF)
    grad_reduce = over_rows(hidden, grad_branch)
    grad_hidden = against_rows(grad_branch, w_reduce)
    _, gelu_back = jax.vjp(gelu_tanh, expanded)
    grad_expanded = gelu_back(grad_hidden)[0].astype(BF)
    grad_expand = over_rows(normed_two, grad_expanded)
    grad_normed = against_rows(grad_expanded, w_expand)
    _, norm_back = jax.vjp(layer_norm, middle, gain_two)
    grad_part, grad_gain_two = norm_back(grad_normed)
    grad_middle = grad_out + grad_part
    grad_branch = grad_middle.astype(BF)
    grad_mixing = over_rows(mixed, grad_branch)
    grad_mixed = against_rows(grad_branch, w_mixing).astype(BF)
    grad_triple = attend_back(triple, exact, grad_mixed, chips, heads)
    grad_weights = over_rows(normed_one, grad_triple)
    grad_normed = against_rows(grad_triple, w_triple)
    _, norm_back = jax.vjp(layer_norm, rows, gain_one)
    grad_part, grad_gain_one = norm_back(grad_normed)
    return (
        grad_middle + grad_part,
        (grad_weights, grad_mixing, grad_expand, grad_reduce),
        (grad_gain_one, grad_gain_two),
    )


class Cube:
    def __init__(self):
        self.dims = {}
        self.names = []
        for axis in ("section", "dp"):
            bits = (lax.axis_size(axis) - 1).bit_length()
            for bit in reversed(range(bits)):
                name = (axis, bit)
                self.names.append(name)
                self.dims[name] = (lax.axis_index(axis) >> bit) & 1
        z = [("dp", bit) for bit in range(2, len(self.names) - 1)]
        first, second, core = ("dp", 1), ("section", 0), ("dp", 0)
        self.orders = (z + [first, second, core], z + [second, first, core])

    def swap(self, value, name):
        axis, bit = name
        route = [(i, i ^ (1 << bit)) for i in range(lax.axis_size(axis))]
        return lax.ppermute(value, axis, route)

    def gather(self, piece, order):
        held = []
        value = piece
        lead = 0
        for name in order:
            got = self.swap(value, name)
            place = sum(1 for other in held if self.names.index(other) < self.names.index(name))
            mine = self.dims[name] == 0
            value = jnp.where(
                mine, jnp.stack([value, got], place), jnp.stack([got, value], place)
            )
            held.append(name)
            lead += 1
        return value.reshape((1 << lead,) + piece.shape)

    def scatter(self, value, order):
        held = list(self.names)
        tail = value.shape[1:]
        value = value.reshape((2,) * len(held) + tail)
        for name in reversed(order):
            place = held.index(name)
            mine = self.dims[name]
            away = lax.dynamic_index_in_dim(value, 1 - mine, place, keepdims=False)
            here = lax.dynamic_index_in_dim(value, mine, place, keepdims=False)
            got = self.swap(away, name)
            total = here.astype(F32) + got.astype(F32)
            held.remove(name)
            value = total.astype(BF) if held else total
        return value


def stacked(shard, width):
    return jnp.concatenate(
        [shard[:, i : i + width] for i in range(0, shard.shape[1], width)], axis=0
    )


def pack(shards, width):
    return jnp.concatenate([stacked(shard, width) for shard in shards], axis=0)


def unpack(full, shards, width):
    out = []
    at = 0
    for rows, columns in shards:
        parts = columns // width
        blocks = [full[:, at + i * rows : at + (i + 1) * rows] for i in range(parts)]
        at += parts * rows
        whole = blocks[0] if parts == 1 else jnp.concatenate(blocks, axis=2)
        out.append(whole.reshape(full.shape[0] * rows, columns))
    return out


def pack_whole(grads, shards, width, devices):
    blocks = []
    for grad, (rows, columns) in zip(grads, shards):
        split = grad.astype(BF).reshape(devices, rows, columns)
        blocks += [split[:, :, i : i + width] for i in range(0, columns, width)]
    return jnp.concatenate(blocks, axis=1)


def unpack_shard(piece, shards, width):
    out = []
    at = 0
    for rows, columns in shards:
        blocks = []
        for _ in range(columns // width):
            blocks.append(piece[at : at + rows])
            at += rows
        out.append(blocks[0] if len(blocks) == 1 else jnp.concatenate(blocks, axis=1))
    return out


def local(
    tokens,
    patch_order,
    sensor_tag,
    class_token,
    sensor_table,
    enc_gain_one,
    enc_qkv,
    enc_out,
    enc_gain_two,
    enc_up,
    enc_down,
    dec_proj,
    mask_token,
    dec_gain_one,
    dec_qkv,
    dec_out,
    dec_gain_two,
    dec_up,
    dec_down,
    out_grad,
):
    cube = Cube()
    devices = lax.axis_size("section") * lax.axis_size("dp")
    section = lax.axis_index("section")
    sections = lax.axis_size("section")
    width_enc = tokens.shape[1]
    width_dec = out_grad.shape[1]
    groups = (
        ((enc_qkv, enc_out), width_enc, 0),
        ((enc_up,), width_enc, 1),
        ((enc_down,), width_enc, 0),
        ((dec_proj, dec_qkv, dec_out), width_dec, 1),
        ((dec_up, dec_down), width_dec, 0),
    )
    shapes = [[shard.shape for shard in group] for group, _, _ in groups]
    full = []
    for (group, width, way), shape in zip(groups, shapes):
        whole = cube.gather(pack(group, width), cube.orders[way])
        full += unpack(whole, shape, width)
    enc_weights = (
        enc_gain_one.astype(F32),
        full[0],
        full[1],
        enc_gain_two.astype(F32),
        full[2],
        full[3],
    )
    projection = full[4]
    dec_weights = (
        dec_gain_one.astype(F32),
        full[5],
        full[6],
        dec_gain_two.astype(F32),
        full[7],
        full[8],
    )
    chips_all = patch_order.shape[0]
    chips = chips_all // sections
    seq_in = tokens.shape[0] // chips_all
    seq_out = patch_order.shape[1]
    visible_count = seq_in - 1
    sensor_count = sensor_table.shape[0]

    def mine(whole):
        rows = whole.shape[0] // sections
        return lax.dynamic_slice_in_dim(whole, section * rows, rows, axis=0)

    tok_rows, tags, order, grad_rows = (
        mine(tokens),
        mine(sensor_tag),
        mine(patch_order),
        mine(out_grad),
    )
    table = position_table(seq_out, width_dec)
    places = jnp.arange(seq_out, dtype=jnp.int32)
    onehot = tags[:, None] == jnp.arange(sensor_count, dtype=jnp.int32)[None, :]
    sensor_rows = matmul(onehot.astype(BF), sensor_table)
    lead = jnp.broadcast_to(class_token.astype(F32)[None, None, :], (chips, 1, width_enc))
    sequence = (
        jnp.concatenate([lead, tok_rows.astype(F32).reshape(chips, seq_in, width_enc)], axis=1)
        + sensor_rows[:, None, :]
    ).reshape(chips * (seq_in + 1), width_enc)

    encoded, enc_kept = block_forward(sequence, enc_weights, chips, HEADS_E)
    visible = encoded.reshape(chips, seq_in + 1, width_enc)[:, 2:].astype(BF)

    projected = matmul(visible.reshape(-1, width_enc), projection).reshape(
        chips, visible_count, width_dec
    )
    chosen = places[None, :, None] == order[:, None, :visible_count]
    seen = jnp.any(chosen, axis=2)[:, :, None]
    high = projected.astype(BF)
    low = (projected - high.astype(F32)).astype(BF)
    picked = jnp.einsum(
        "cpj,cjd->cpd",
        jnp.concatenate([chosen, chosen], axis=2).astype(BF),
        jnp.concatenate([high, low], axis=1),
        preferred_element_type=F32,
    )
    decoder_in = (
        jnp.where(seen, picked, mask_token.astype(F32)[None, None, :]) + table[None, :, :]
    )
    decoded, dec_kept = block_forward(
        decoder_in.reshape(-1, width_dec), dec_weights, chips, HEADS_D
    )
    grad_in, dec_matrices, dec_gains = block_back(
        dec_kept, grad_rows.astype(F32), dec_weights, chips, HEADS_D
    )
    grad_chip = grad_in.reshape(chips, seq_out, width_dec)
    mask_grad = jnp.sum(jnp.where(seen, 0.0, grad_chip), axis=(0, 1))
    grad_projected = (
        jnp.einsum(
            "cpj,cpd->cjd", chosen.astype(BF), grad_chip.astype(BF), preferred_element_type=F32
        )
        .astype(BF)
        .reshape(chips * visible_count, width_dec)
    )
    proj_grad = over_rows(visible.reshape(-1, width_enc), grad_projected)
    grad_visible = against_rows(grad_projected, projection).astype(BF)

    grad_encoded = jnp.pad(
        grad_visible.astype(F32).reshape(chips, visible_count, width_enc),
        ((0, 0), (2, 0), (0, 0)),
    )
    grad_sequence, enc_matrices, enc_gains = block_back(
        enc_kept, grad_encoded.reshape(-1, width_enc), enc_weights, chips, HEADS_E
    )
    grad_seq = grad_sequence.reshape(chips, seq_in + 1, width_enc)
    sensor_grad = jnp.sum(
        jnp.where(onehot[:, :, None], jnp.sum(grad_seq, axis=1)[:, None, :], 0.0), axis=0
    )
    class_grad = jnp.sum(grad_seq[:, 0], axis=0)
    token_rows = grad_seq[:, 1:].reshape(chips * seq_in, width_enc)

    grads = (
        (enc_matrices[0], enc_matrices[1]),
        (enc_matrices[2],),
        (enc_matrices[3],),
        (proj_grad, dec_matrices[0], dec_matrices[1]),
        (dec_matrices[2], dec_matrices[3]),
    )
    sums = [None] * len(groups)
    for index in (4, 3, 2, 1, 0):
        _, width, way = groups[index]
        whole = pack_whole(grads[index], shapes[index], width, devices)
        piece = cube.scatter(whole, cube.orders[way])
        sums[index] = unpack_shard(piece, shapes[index], width)
    big = [value for group in sums for value in group]

    small = lax.psum(
        (class_grad, sensor_grad) + enc_gains + (mask_grad,) + dec_gains, ("section", "dp")
    )

    def halves(rows):
        half = rows.shape[1] // sections
        own = lax.dynamic_slice_in_dim(rows, section * half, half, axis=1)
        away = lax.dynamic_slice_in_dim(rows, (1 - section) * half, half, axis=1)
        got = cube.swap(away.astype(BF), ("section", 0)).astype(rows.dtype)
        return jnp.where(
            section == 0, jnp.concatenate([own, got], 0), jnp.concatenate([got, own], 0)
        )

    return (halves(decoded.astype(BF)), halves(token_rows)) + tuple(big) + tuple(small)


def solution(mesh):
    every = P(("section", "dp"), None)
    rows = P("dp", None)
    in_specs = (
        rows,
        rows,
        P("dp"),
        P(),
        P(),
        P(),
        every,
        every,
        P(),
        every,
        every,
        every,
        P(),
        P(),
        every,
        every,
        P(),
        every,
        every,
        rows,
    )
    out_specs = (P("dp", "section"),) * 2 + (every,) * 9 + (P(),) * 7
    return jax.shard_map(local, mesh=mesh, in_specs=in_specs, out_specs=out_specs, check_vma=False)
```

time: 1770 us -> 581 us (0.33)
  waiting for transfers between devices: 1160 us -> 230 us
  matrix products: 179 us -> 69.7 us
  blocking collectives: 130 us -> 39.4 us
  other arithmetic: 128 us -> 59.2 us
  starting transfers between devices: 15 us -> 59.4 us
  loops' own time: 27.2 us -> 0 us
    reduce_scatter x9 -> x0, waiting for transfers between devices: 767 us -> none  [local(): lax.psum_scatter(big_total, ('section', 'dp'), scatter_dimension=0, tiled...]
    all_gather x7 -> x0, waiting for transfers between devices: 253 us -> none  [the longest x1 65.3 us: local(): lax.all_gather(enc_up, ('section', 'dp'), axis=0, tiled=True)]
    add x18 -> x7, other arithmetic: 93.3 us -> 1.77 us  [the longest x1 0.91 us: block_back(): grad_middle + grad_part]
    ppermute x10 -> x52, waiting for transfers between devices: 140 us -> 230 us  [swap(): return lax.ppermute(value, axis, route)]
    all_gather x2 -> x0, blocking collectives: 84.5 us -> none  [the longest x1 44.9 us: local(): lax.all_gather(dec_out, ('section', 'dp'), axis=0, tiled=True)]
    dot_general x44 -> x18, matrix products: 78.5 us -> 19.7 us  [the longest x10 10.8 us: matmul(): return jnp.dot(left, right, preferred_element_type=F32)]
    ppermute x10 -> x52, starting transfers between devices: 14.3 us -> 59.4 us  [swap(): return lax.ppermute(value, axis, route)]
    another operation x44 -> x2, local copies, waits for them, and re-layouts: 31.2 us -> 3.57 us  [attend_back(): grad_triple = jnp.stack([grad_query, grad_key, grad_value], axis=2)]
  transfers between devices with their start and end apart: 26 -> 52, of which waited for: 12 -> 22; matrix products, arithmetic and copies ran while one was open for 20% -> 13% of each run, Pallas kernels for 0% -> 0%
where the time goes in v1:
time: 581 us; the launch traced here: 570 us
  waiting for transfers between devices  230 us (40%)
  local copies, waits for them, and re-layouts  109 us (19%)
  matrix products  69.7 us (12%)
  starting transfers between devices  59.4 us (10%)
  other arithmetic  59.2 us (10%)
  blocking collectives  39.4 us (7%)
    ppermute x52, waiting for transfers between devices, swap(): return lax.ppermute(value, axis, route)  230 us
    ppermute x52, starting transfers between devices, swap(): return lax.ppermute(value, axis, route)  59.4 us
    unnamed x236, local copies, waits for them, and re-layouts  43.4 us
    psum x1, blocking collectives, local(): lax.psum((class_grad, sensor_grad) + enc_gains + (mask_grad,) + dec_gains...  39.4 us
    dot_general x9, matrix products, over_rows(): lax.dot_general(left, right, (((0,), (0,)), ((), ())), preferred_element_...  22.4 us
    dot_general x9, matrix products, against_rows(): lax.dot_general(left, right, (((1,), (1,)), ((), ())), preferred_element_...  19.3 us
    select_n x45, other arithmetic, gather(): jnp.where(mine, jnp.stack([value, got], place), jnp.stack([got, value], p...  16.7 us
    convert_element_type x20, other arithmetic, scatter(): value = total.astype(BF) if held else total  12.3 us
  transfers between devices with their start and end apart: 52, of which 22 were waited for; matrix products, arithmetic and copies ran while one was open for 13% of the time, Pallas kernels for 0%

profile of v1, /device:TPU:0, one launch (start us, length us, event | category | flops | bytes accessed | tf_op | source)
XLA Modules:
  0.0 569.7 jit_solution(9113026562261076747)
XLA Ops:
  4.4 3.0 collective-permute-start.15
  24.2 2.7 collective-permute-start.16
  27.6 2.7 collective-permute-start.6
  30.8 2.7 collective-permute-start.1
  33.5 26.2 %collective-permute-done.16 = bf16[2,88,512]{2,1,0:T(8,128)(2,1)S(1)} collective-permute-done((bf16[2,88,512]{2,1,0:T(8,128)(2,1)S(1)}, bf16[2,88,512]{2,1,0:T(8,128)(2,1)S(1)}, u32[]{:S(2)}, u32[]{:S(2)}) %collective-permute-start.16) | collective-permute-done | bytes 180256 | tf_op jit(solution)/shard_map/ppermute | solution.py:149
  61.5 3.9 collective-permute-done.21
  67.2 15.8 %collective-permute-done.1 = bf16[2,96,768]{2,1,0:T(8,128)(2,1)S(1)} collective-permute-done((bf16[2,96,768]{2,1,0:T(8,128)(2,1)S(1)}, bf16[2,96,768]{2,1,0:T(8,128)(2,1)S(1)}, u32[]{:S(2)}, u32[]{:S(2)}) %collective-permute-start.1) | collective-permute-done | bytes 294944 | tf_op jit(solution)/shard_map/ppermute | solution.py:149
  90.6 11.4 %collective-permute-done.7 = bf16[2,2,96,768]{3,2,1,0:T(8,128)(2,1)S(1)} collective-permute-done((bf16[2,2,96,768]{3,2,1,0:T(8,128)(2,1)S(1)}, bf16[2,2,96,768]{3,2,1,0:T(8,128)(2,1)S(1)}, u32[]{:S(2)}, u32[]{:S(2)}) %collective-permute-start.7) | collective-permute-done | bytes 589856 | tf_op jit(solution)/shard_map/ppermute | solution.py:149
  103.8 8.3 %collective-permute-done.12 = bf16[2,2,96,768]{3,2,1,0:T(8,128)(2,1)S(1)} collective-permute-done((bf16[2,2,96,768]{3,2,1,0:T(8,128)(2,1)S(1)}, bf16[2,2,96,768]{3,2,1,0:T(8,128)(2,1)S(1)}, u32[]{:S(2)}, u32[]{:S(2)}) %collective-permute-start.12) | collective-permute-done | bytes 589856 | tf_op jit(solution)/shard_map/ppermute | solution.py:149
  115.7 11.8 %collective-permute-done.18 = bf16[2,2,2,88,512]{4,3,2,1,0:T(8,128)(2,1)S(1)} collective-permute-done((bf16[2,2,2,88,512]{4,3,2,1,0:T(8,128)(2,1)S(1)}, bf16[2,2,2,88,512]{4,3,2,1,0:T(8,128)(2,1)S(1)}, u32[]{:S(2)}, u32[]{:S(2)}) %collective-permute-start.18) | collective-permute-done | bytes 720928 | tf_op jit(solution)/shard_map/ppermute | solution.py:149
  130.7 41.6 %collective-permute-done.3 = bf16[2,2,2,96,768]{4,3,2,1,0:T(8,128)(2,1)S(1)} collective-permute-done((bf16[2,2,2,96,768]{4,3,2,1,0:T(8,128)(2,1)S(1)}, bf16[2,2,2,96,768]{4,3,2,1,0:T(8,128)(2,1)S(1)}, u32[]{:S(2)}, u32[]{:S(2)}) %collective-permute-start.3) | collective-permute-done | bytes 1179680 | tf_op jit(solution)/shard_map/ppermute | solution.py:149
  180.0 2.8 maximum_select_fusion.3
  186.1 3.2 maximum_select_fusion.2
  189.3 2.6 copy.145
  199.8 3.1 reshape.2682
  202.9 2.8 fusion.139
  219.0 2.6 pad_maximum_fusion
  232.1 5.0 reshape.2737
  237.1 3.6 fusion.136
  240.7 2.5 copy.207
  245.7 2.5 copy.208
  250.2 3.2 fusion.154
  262.0 4.4 fusion.8
  266.4 3.2 convolution_convert_fusion.6
  271.6 2.8 convolution_convert_fusion.7
  278.6 2.6 reshape.2738
  281.2 2.5 copy.163
  283.7 3.3 fusion.41
  301.4 5.3 fusion.26
  318.9 3.9 convolution_convert_fusion
  322.8 3.7 convolution_convert_fusion.1
  369.7 39.4 %all-reduce.1 = (f32[768]{0:T(1024)}, f32[8,768]{1,0:T(8,128)}, f32[768]{0:T(1024)}, f32[768]{0:T(1024)}, f32[512]{0:T(512)}, /*index=5*/f32[512]{0:T(512)}, f32[512]{0:T(512)}) all-reduce(f32[768]{0:T(1024)S(1)} %slice_reduce_fusion, f32[8,768]{1,0:T(8,128)S(1)} %select_reduce_fusion.1, ...), channel_id=1, replica_groups=mesh['section'=2,'dp'=16] {'section','dp'}, use_global_device_ids=true, to_apply=%region_24.25 | all-reduce | flops 9984 | bytes 79872 | tf_op jit(solution)/shard_map/psum | solution.py:374
  422.4 8.9 %collective-permute-done.43 = bf16[2,2,2,88,512]{4,3,2,1,0:T(8,128)(2,1)S(1)} collective-permute-done((bf16[2,2,2,88,512]{4,3,2,1,0:T(8,128)(2,1)S(1)}, bf16[2,2,2,88,512]{4,3,2,1,0:T(8,128)(2,1)S(1)}, u32[]{:S(2)}, u32[]{:S(2)}) %collective-permute-start.43) | collective-permute-done | bytes 720928 | tf_op jit(solution)/shard_map/ppermute | solution.py:149
  436.3 2.5 fusion.2
  439.5 14.8 %collective-permute-done.44 = bf16[2,2,88,512]{3,2,1,0:T(8,128)(2,1)S(1)} collective-permute-done((bf16[2,2,88,512]{3,2,1,0:T(8,128)(2,1)S(1)}, bf16[2,2,88,512]{3,2,1,0:T(8,128)(2,1)S(1)}, u32[]{:S(2)}, u32[]{:S(2)}) %collective-permute-start.44) | collective-permute-done | bytes 360480 | tf_op jit(solution)/shard_map/ppermute | solution.py:149
  454.5 3.0 collective-permute-start.45
  458.2 7.2 %collective-permute-done.45 = bf16[2,88,512]{2,1,0:T(8,128)(2,1)S(1)} collective-permute-done((bf16[2,88,512]{2,1,0:T(8,128)(2,1)S(1)}, bf16[2,88,512]{2,1,0:T(8,128)(2,1)S(1)}, u32[]{:S(2)}, u32[]{:S(2)}) %collective-permute-start.45) | collective-permute-done | bytes 180256 | tf_op jit(solution)/shard_map/ppermute | solution.py:149
  467.5 2.6 collective-permute-done.46
  474.2 5.5 collective-permute-done.28
  481.8 24.1 %collective-permute-done.49 = bf16[2,2,128,512]{3,2,1,0:T(8,128)(2,1)S(1)} collective-permute-done((bf16[2,2,128,512]{3,2,1,0:T(8,128)(2,1)S(1)}, bf16[2,2,128,512]{3,2,1,0:T(8,128)(2,1)S(1)}, u32[]{:S(2)}, u32[]{:S(2)}) %collective-permute-start.49) | collective-permute-done | bytes 524320 | tf_op jit(solution)/shard_map/ppermute | solution.py:149
  510.4 6.1 %collective-permute-done.50 = bf16[2,128,512]{2,1,0:T(8,128)(2,1)S(1)} collective-permute-done((bf16[2,128,512]{2,1,0:T(8,128)(2,1)S(1)}, bf16[2,128,512]{2,1,0:T(8,128)(2,1)S(1)}, u32[]{:S(2)}, u32[]{:S(2)}) %collective-permute-start.50) | collective-permute-done | bytes 262176 | tf_op jit(solution)/shard_map/ppermute | solution.py:149
  519.1 2.5 collective-permute-done.51
  523.7 5.1 collective-permute-done.39
  532.3 16.9 %collective-permute-done.30 = bf16[2,96,768]{2,1,0:T(8,128)(2,1)S(1)} collective-permute-done((bf16[2,96,768]{2,1,0:T(8,128)(2,1)S(1)}, bf16[2,96,768]{2,1,0:T(8,128)(2,1)S(1)}, u32[]{:S(2)}, u32[]{:S(2)}) %collective-permute-start.30) | collective-permute-done | bytes 294944 | tf_op jit(solution)/shard_map/ppermute | solution.py:149
  549.4 6.2 %collective-permute-done.40 = bf16[2,96,768]{2,1,0:T(8,128)(2,1)S(1)} collective-permute-done((bf16[2,96,768]{2,1,0:T(8,128)(2,1)S(1)}, bf16[2,96,768]{2,1,0:T(8,128)(2,1)S(1)}, u32[]{:S(2)}, u32[]{:S(2)}) %collective-permute-start.40) | collective-permute-done | bytes 294944 | tf_op jit(solution)/shard_map/ppermute | solution.py:149
  555.8 3.6 collective-permute-done.35
  559.6 2.8 collective-permute-done.31
  563.1 4.1 collective-permute-done.36
  (576 shorter events, 215.3 us)
Async XLA Ops:
  4.4 19.8 %collective-permute-start.15 = (bf16[88,512]{1,0:T(8,128)(2,1)S(1)}, bf16[88,512]{1,0:T(8,128)(2,1)S(1)}, u32[]{:S(2)}, u32[]{:S(2)}) collective-permute-start(bf16[88,512]{1,0:T(8,128)(2,1)S(1)} %constant_dynamic-update-slice_fusion), channel_id=1, source_target_pairs={{0,4},{1,5},{2,6},{3,7},{4,0},{5,1},{6,2},{7,3},{8,12},{9,13},{10,... | collective-permute-start | bytes 270344 | tf_op jit(solution)/shard_map/ppermute | solution.py:149
  11.1 15.8 %collective-permute-start.20 = (bf16[128,512]{1,0:T(8,128)(2,1)S(1)}, bf16[128,512]{1,0:T(8,128)(2,1)S(1)}, u32[]{:S(2)}, u32[]{:S(2)}) collective-permute-start(bf16[128,512]{1,0:T(8,128)(2,1)S(1)} %constant_dynamic-update-slice_fusion.5), channel_id=1, source_target_pairs={{0,4},{1,5},{2,6},{3,7},{4,0},{5,1},{6,2},{7,3},{8,12},{9,13},{10,... | collective-permute-start | bytes 393224 | tf_op jit(solution)/shard_map/ppermute | solution.py:149
  11.1 16.3 %collective-permute-start.10 = (bf16[96,768]{1,0:T(8,128)(2,1)}, bf16[96,768]{1,0:T(8,128)(2,1)S(1)}, u32[]{:S(2)}, u32[]{:S(2)}) collective-permute-start(bf16[96,768]{1,0:T(8,128)(2,1)} %param.30), channel_id=1, source_target_pairs={{0,4},{1,5},{2,6},{3,7},{4,0},{5,1},{6,2},{7,3},{8,12},{9,13},{10,... | collective-permute-start | bytes 442376 | tf_op jit(solution)/shard_map/ppermute | solution.py:149
  14.0 13.5 %collective-permute-start.5 = (bf16[96,768]{1,0:T(8,128)(2,1)S(1)}, bf16[96,768]{1,0:T(8,128)(2,1)S(1)}, u32[]{:S(2)}, u32[]{:S(2)}) collective-permute-start(bf16[96,768]{1,0:T(8,128)(2,1)S(1)} %get-tuple-element.115), channel_id=1, source_target_pairs={{0,4},{1,5},{2,6},{3,7},{4,0},{5,1},{6,2},{7,3},{8,12},{9,13},{10,... | collective-permute-start | bytes 442376 | tf_op jit(solution)/shard_map/ppermute | solution.py:149
  15.8 15.0 %collective-permute-start = (bf16[96,768]{1,0:T(8,128)(2,1)S(1)}, bf16[96,768]{1,0:T(8,128)(2,1)S(1)}, u32[]{:S(2)}, u32[]{:S(2)}) collective-permute-start(bf16[96,768]{1,0:T(8,128)(2,1)S(1)} %get-tuple-element.122), channel_id=1, source_target_pairs={{0,4},{1,5},{2,6},{3,7},{4,0},{5,1},{6,2},{7,3},{8,12},{9,13},{10,... | collective-permute-start | bytes 442376 | tf_op jit(solution)/shard_map/ppermute | solution.py:149
  24.2 35.6 %collective-permute-start.16 = (bf16[2,88,512]{2,1,0:T(8,128)(2,1)S(1)}, bf16[2,88,512]{2,1,0:T(8,128)(2,1)S(1)}, u32[]{:S(2)}, u32[]{:S(2)}) collective-permute-start(bf16[2,88,512]{2,1,0:T(8,128)(2,1)S(1)} %maximum_select_fusion.38), channel_id=1, source_target_pairs={{0,8},{1,9},{2,10},{3,11},{4,12},{5,13},{6,14},{7,15},{8,0},{9,1},... | collective-permute-start | bytes 540680 | tf_op jit(solution)/shard_map/ppermute | solution.py:149
  27.0 38.4 %collective-permute-start.21 = (bf16[2,128,512]{2,1,0:T(8,128)(2,1)S(1)}, bf16[2,128,512]{2,1,0:T(8,128)(2,1)S(1)}, u32[]{:S(2)}, u32[]{:S(2)}) collective-permute-start(bf16[2,128,512]{2,1,0:T(8,128)(2,1)S(1)} %maximum_select_fusion.36), channel_id=1, source_target_pairs={{0,8},{1,9},{2,10},{3,11},{4,12},{5,13},{6,14},{7,15},{8,0},{9,1},... | collective-permute-start | bytes 786440 | tf_op jit(solution)/shard_map/ppermute | solution.py:149
  27.6 58.0 %collective-permute-start.6 = (bf16[2,96,768]{2,1,0:T(8,128)(2,1)S(1)}, bf16[2,96,768]{2,1,0:T(8,128)(2,1)S(1)}, u32[]{:S(2)}, u32[]{:S(2)}) collective-permute-start(bf16[2,96,768]{2,1,0:T(8,128)(2,1)S(1)} %maximum_select_fusion.32), channel_id=1, source_target_pairs={{0,8},{1,9},{2,10},{3,11},{4,12},{5,13},{6,14},{7,15},{8,0},{9,1},... | collective-permute-start | bytes 884744 | tf_op jit(solution)/shard_map/ppermute | solution.py:149
  30.3 54.4 %collective-permute-start.11 = (bf16[2,96,768]{2,1,0:T(8,128)(2,1)S(1)}, bf16[2,96,768]{2,1,0:T(8,128)(2,1)S(1)}, u32[]{:S(2)}, u32[]{:S(2)}) collective-permute-start(bf16[2,96,768]{2,1,0:T(8,128)(2,1)S(1)} %maximum_select_fusion.34), channel_id=1, source_target_pairs={{0,8},{1,9},{2,10},{3,11},{4,12},{5,13},{6,14},{7,15},{8,0},{9,1},... | collective-permute-start | bytes 884744 | tf_op jit(solution)/shard_map/ppermute | solution.py:149
  30.8 52.2 %collective-permute-start.1 = (bf16[2,96,768]{2,1,0:T(8,128)(2,1)S(1)}, bf16[2,96,768]{2,1,0:T(8,128)(2,1)S(1)}, u32[]{:S(2)}, u32[]{:S(2)}) collective-permute-start(bf16[2,96,768]{2,1,0:T(8,128)(2,1)S(1)} %maximum_select_fusion.30), channel_id=1, source_target_pairs={{0,8},{1,9},{2,10},{3,11},{4,12},{5,13},{6,14},{7,15},{8,0},{9,1},... | collective-permute-start | bytes 884744 | tf_op jit(solution)/shard_map/ppermute | solution.py:149
  59.8 27.8 %collective-permute-start.17 = (bf16[2,2,88,512]{3,2,1,0:T(8,128)(2,1)S(1)}, bf16[2,2,88,512]{3,2,1,0:T(8,128)(2,1)S(1)}, u32[]{:S(2)}, u32[]{:S(2)}) collective-permute-start(bf16[2,2,88,512]{3,2,1,0:T(8,128)(2,1)S(1)} %maximum_select_fusion.28), channel_id=1, source_target_pairs={{0,16},{16,0},{1,17},{17,1},{2,18},{18,2},{3,19},{19,3},{4,20},{20... | collective-permute-start | bytes 1081352 | tf_op jit(solution)/shard_map/ppermute | solution.py:149
  65.5 24.1 %collective-permute-start.22 = (bf16[2,2,128,512]{3,2,1,0:T(8,128)(2,1)S(1)}, bf16[2,2,128,512]{3,2,1,0:T(8,128)(2,1)S(1)}, u32[]{:S(2)}, u32[]{:S(2)}) collective-permute-start(bf16[2,2,128,512]{3,2,1,0:T(8,128)(2,1)S(1)} %maximum_select_fusion.24), channel_id=1, source_target_pairs={{0,2},{1,3},{2,0},{3,1},{4,6},{5,7},{6,4},{7,5},{8,10},{9,11},{10,... | collective-permute-start | bytes 1572872 | tf_op jit(solution)/shard_map/ppermute | solution.py:149
  83.1 31.2 %collective-permute-start.2 = (bf16[2,2,96,768]{3,2,1,0:T(8,128)(2,1)S(1)}, bf16[2,2,96,768]{3,2,1,0:T(8,128)(2,1)S(1)}, u32[]{:S(2)}, u32[]{:S(2)}) collective-permute-start(bf16[2,2,96,768]{3,2,1,0:T(8,128)(2,1)S(1)} %maximum_select_fusion.19), channel_id=1, source_target_pairs={{0,2},{1,3},{2,0},{3,1},{4,6},{5,7},{6,4},{7,5},{8,10},{9,11},{10,... | collective-permute-start | bytes 1769480 | tf_op jit(solution)/shard_map/ppermute | solution.py:149
  84.8 27.3 %collective-permute-start.12 = (bf16[2,2,96,768]{3,2,1,0:T(8,128)(2,1)S(1)}, bf16[2,2,96,768]{3,2,1,0:T(8,128)(2,1)S(1)}, u32[]{:S(2)}, u32[]{:S(2)}) collective-permute-start(bf16[2,2,96,768]{3,2,1,0:T(8,128)(2,1)S(1)} %maximum_select_fusion.23), channel_id=1, source_target_pairs={{0,2},{1,3},{2,0},{3,1},{4,6},{5,7},{6,4},{7,5},{8,10},{9,11},{10,... | collective-permute-start | bytes 1769480 | tf_op jit(solution)/shard_map/ppermute | solution.py:149
  85.7 16.3 %collective-permute-start.7 = (bf16[2,2,96,768]{3,2,1,0:T(8,128)(2,1)S(1)}, bf16[2,2,96,768]{3,2,1,0:T(8,128)(2,1)S(1)}, u32[]{:S(2)}, u32[]{:S(2)}) collective-permute-start(bf16[2,2,96,768]{3,2,1,0:T(8,128)(2,1)S(1)} %maximum_select_fusion.21), channel_id=1, source_target_pairs={{0,16},{16,0},{1,17},{17,1},{2,18},{18,2},{3,19},{19,3},{4,20},{20... | collective-permute-start | bytes 1769480 | tf_op jit(solution)/shard_map/ppermute | solution.py:149
  87.8 39.7 %collective-permute-start.18 = (bf16[2,2,2,88,512]{4,3,2,1,0:T(8,128)(2,1)S(1)}, bf16[2,2,2,88,512]{4,3,2,1,0:T(8,128)(2,1)S(1)}, u32[]{:S(2)}, u32[]{:S(2)}) collective-permute-start(bf16[2,2,2,88,512]{4,3,2,1,0:T(8,128)(2,1)S(1)} %maximum_select_fusion.18), channel_id=1, source_target_pairs={{0,2},{1,3},{2,0},{3,1},{4,6},{5,7},{6,4},{7,5},{8,10},{9,11},{10,... | collective-permute-start | bytes 2162696 | tf_op jit(solution)/shard_map/ppermute | solution.py:149
  89.7 38.5 %collective-permute-start.23 = (bf16[2,2,2,128,512]{4,3,2,1,0:T(8,128)(2,1)S(1)}, bf16[2,2,2,128,512]{4,3,2,1,0:T(8,128)(2,1)S(1)}, u32[]{:S(2)}, u32[]{:S(2)}) collective-permute-start(bf16[2,2,2,128,512]{4,3,2,1,0:T(8,128)(2,1)S(1)} %maximum_select_fusion.17), channel_id=1, source_target_pairs={{0,16},{16,0},{1,17},{17,1},{2,18},{18,2},{3,19},{19,3},{4,20},{20... | collective-permute-start | bytes 3145736 | tf_op jit(solution)/shard_map/ppermute | solution.py:149
  102.2 71.4 %collective-permute-start.8 = (bf16[2,2,2,96,768]{4,3,2,1,0:T(8,128)(2,1)S(1)}, bf16[2,2,2,96,768]{4,3,2,1,0:T(8,128)(2,1)S(1)}, u32[]{:S(2)}, u32[]{:S(2)}) collective-permute-start(bf16[2,2,2,96,768]{4,3,2,1,0:T(8,128)(2,1)S(1)} %maximum_select_fusion.14), channel_id=1, source_target_pairs={{0,2},{1,3},{2,0},{3,1},{4,6},{5,7},{6,4},{7,5},{8,10},{9,11},{10,... | collective-permute-start | bytes 3538952 | tf_op jit(solution)/shard_map/ppermute | solution.py:149
  112.3 60.4 %collective-permute-start.13 = (bf16[2,2,2,96,768]{4,3,1,0,2:T(8,128)(2,1)S(1)}, bf16[2,2,2,96,768]{4,3,1,0,2:T(8,128)(2,1)S(1)}, u32[]{:S(2)}, u32[]{:S(2)}) collective-permute-start(bf16[2,2,2,96,768]{4,3,1,0,2:T(8,128)(2,1)S(1)} %maximum_select_fusion.16), channel_id=1, source_target_pairs={{0,16},{16,0},{1,17},{17,1},{2,18},{18,2},{3,19},{19,3},{4,20},{20... | collective-permute-start | bytes 3538952 | tf_op jit(solution)/shard_map/ppermute | solution.py:149
  114.4 57.8 %collective-permute-start.3 = (bf16[2,2,2,96,768]{4,3,2,1,0:T(8,128)(2,1)S(1)}, bf16[2,2,2,96,768]{4,3,2,1,0:T(8,128)(2,1)S(1)}, u32[]{:S(2)}, u32[]{:S(2)}) collective-permute-start(bf16[2,2,2,96,768]{4,3,2,1,0:T(8,128)(2,1)S(1)} %maximum_select_fusion.12), channel_id=1, source_target_pairs={{0,16},{16,0},{1,17},{17,1},{2,18},{18,2},{3,19},{19,3},{4,20},{20... | collective-permute-start | bytes 3538952 | tf_op jit(solution)/shard_map/ppermute | solution.py:149
  127.7 47.8 %collective-permute-start.19 = (bf16[2,2,2,2,88,512]{5,4,3,2,1,0:T(8,128)(2,1)S(1)}, bf16[2,2,2,2,88,512]{5,4,3,2,1,0:T(8,128)(2,1)}, u32[]{:S(2)}, u32[]{:S(2)}) collective-permute-start(bf16[2,2,2,2,88,512]{5,4,3,2,1,0:T(8,128)(2,1)S(1)} %maximum_select_fusion.11), channel_id=1, source_target_pairs={{0,1},{1,0},{2,3},{3,2},{4,5},{5,4},{6,7},{7,6},{8,9},{9,8},{10,11... | collective-permute-start | bytes 4325384 | tf_op jit(solution)/shard_map/ppermute | solution.py:149
  129.8 50.2 %collective-permute-start.24 = (bf16[2,2,2,2,128,512]{5,4,3,2,1,0:T(8,128)(2,1)}, bf16[2,2,2,2,128,512]{5,4,3,2,1,0:T(8,128)(2,1)}, u32[]{:S(2)}, u32[]{:S(2)}) collective-permute-start(bf16[2,2,2,2,128,512]{5,4,3,2,1,0:T(8,128)(2,1)} %maximum_select_fusion.10), channel_id=1, source_target_pairs={{0,1},{1,0},{2,3},{3,2},{4,5},{5,4},{6,7},{7,6},{8,9},{9,8},{10,11... | collective-permute-start | bytes 6291464 | tf_op jit(solution)/shard_map/ppermute | solution.py:149
  172.6 19.3 %collective-permute-start.4 = (bf16[2,2,2,2,96,768]{5,4,3,2,1,0:T(8,128)(2,1)S(1)}, bf16[2,2,2,2,96,768]{5,4,3,2,1,0:T(8,128)(2,1)S(1)}, u32[]{:S(2)}, u32[]{:S(2)}) collective-permute-start(bf16[2,2,2,2,96,768]{5,4,3,2,1,0:T(8,128)(2,1)S(1)} %maximum_select_fusion.5), channel_id=1, source_target_pairs={{0,1},{1,0},{2,3},{3,2},{4,5},{5,4},{6,7},{7,6},{8,9},{9,8},{10,11... | collective-permute-start | bytes 7077896 | tf_op jit(solution)/shard_map/ppermute | solution.py:149
  173.1 13.0 %collective-permute-start.14 = (bf16[2,2,2,2,96,768]{5,4,2,1,3,0:T(8,128)(2,1)S(1)}, bf16[2,2,2,2,96,768]{5,4,2,1,3,0:T(8,128)(2,1)}, u32[]{:S(2)}, u32[]{:S(2)}) collective-permute-start(bf16[2,2,2,2,96,768]{5,4,2,1,3,0:T(8,128)(2,1)S(1)} %maximum_select_fusion.9), channel_id=1, source_target_pairs={{0,1},{1,0},{2,3},{3,2},{4,5},{5,4},{6,7},{7,6},{8,9},{9,8},{10,11... | collective-permute-start | bytes 7077896 | tf_op jit(solution)/shard_map/ppermute | solution.py:149
  174.0 18.7 %collective-permute-start.9 = (bf16[2,2,2,2,96,768]{5,4,2,1,0,3:T(8,128)(2,1)S(1)}, bf16[2,2,2,2,96,768]{5,4,2,1,0,3:T(8,128)(2,1)S(1)}, u32[]{:S(2)}, u32[]{:S(2)}) collective-permute-start(bf16[2,2,2,2,96,768]{5,4,2,1,0,3:T(8,128)(2,1)S(1)} %maximum_select_fusion.7), channel_id=1, source_target_pairs={{0,1},{1,0},{2,3},{3,2},{4,5},{5,4},{6,7},{7,6},{8,9},{9,8},{10,11... | collective-permute-start | bytes 7077896 | tf_op jit(solution)/shard_map/ppermute | solution.py:149
  347.5 61.6 %collective-permute-start.26 = (bf16[130,384]{1,0:T(8,128)(2,1)}, bf16[130,384]{1,0:T(8,128)(2,1)}, u32[]{:S(2)}, u32[]{:S(2)}) collective-permute-start(bf16[130,384]{1,0:T(8,128)(2,1)} %dynamic-slice_convert_fusion), channel_id=1, source_target_pairs={{0,16},{16,0},{1,17},{17,1},{2,18},{18,2},{3,19},{19,3},{4,20},{20... | collective-permute-start | bytes 299528 | tf_op jit(solution)/shard_map/ppermute | solution.py:149
  353.1 59.3 %collective-permute-start.42 = (bf16[2,2,2,2,88,512]{5,4,2,1,0,3:T(8,128)(2,1)}, bf16[2,2,2,2,88,512]{5,4,2,1,0,3:T(8,128)(2,1)}, u32[]{:S(2)}, u32[]{:S(2)}) collective-permute-start(bf16[2,2,2,2,88,512]{5,4,2,1,0,3:T(8,128)(2,1)} %bitcast.468), channel_id=1, source_target_pairs={{0,1},{1,0},{2,3},{3,2},{4,5},{5,4},{6,7},{7,6},{8,9},{9,8},{10,11... | collective-permute-start | bytes 4325384 | tf_op jit(solution)/shard_map/ppermute | solution.py:149
  358.0 74.3 %collective-permute-start.27 = (bf16[2,2,2,2,96,768]{5,4,3,2,1,0:T(8,128)(2,1)}, bf16[2,2,2,2,96,768]{5,4,3,2,1,0:T(8,128)(2,1)}, u32[]{:S(2)}, u32[]{:S(2)}) collective-permute-start(bf16[2,2,2,2,96,768]{5,4,3,2,1,0:T(8,128)(2,1)} %dynamic-slice_bitcast_fusion.1), channel_id=1, source_target_pairs={{0,1},{1,0},{2,3},{3,2},{4,5},{5,4},{6,7},{7,6},{8,9},{9,8},{10,11... | collective-permute-start | bytes 7077896 | tf_op jit(solution)/shard_map/ppermute | solution.py:149
  360.3 76.0 %collective-permute-start.37 = (bf16[2,2,2,2,96,768]{5,4,2,1,3,0:T(8,128)(2,1)}, bf16[2,2,2,2,96,768]{5,4,2,1,3,0:T(8,128)(2,1)}, u32[]{:S(2)}, u32[]{:S(2)}) collective-permute-start(bf16[2,2,2,2,96,768]{5,4,2,1,3,0:T(8,128)(2,1)} %bitcast.466), channel_id=1, source_target_pairs={{0,1},{1,0},{2,3},{3,2},{4,5},{5,4},{6,7},{7,6},{8,9},{9,8},{10,11... | collective-permute-start | bytes 7077896 | tf_op jit(solution)/shard_map/ppermute | solution.py:149
  365.6 52.5 %collective-permute-start.47 = (bf16[2,2,2,2,128,512]{5,4,2,1,3,0:T(8,128)(2,1)}, bf16[2,2,2,2,128,512]{5,4,2,1,3,0:T(8,128)(2,1)}, u32[]{:S(2)}, u32[]{:S(2)}) collective-permute-start(bf16[2,2,2,2,128,512]{5,4,2,1,3,0:T(8,128)(2,1)} %bitcast.467), channel_id=1, source_target_pairs={{0,1},{1,0},{2,3},{3,2},{4,5},{5,4},{6,7},{7,6},{8,9},{9,8},{10,11... | collective-permute-start | bytes 6291464 | tf_op jit(solution)/shard_map/ppermute | solution.py:149
  414.5 16.9 %collective-permute-start.43 = (bf16[2,2,2,88,512]{4,3,2,1,0:T(8,128)(2,1)S(1)}, bf16[2,2,2,88,512]{4,3,2,1,0:T(8,128)(2,1)S(1)}, u32[]{:S(2)}, u32[]{:S(2)}) collective-permute-start(bf16[2,2,2,88,512]{4,3,2,1,0:T(8,128)(2,1)S(1)} %dynamic-slice_bitcast_fusion.6), channel_id=1, source_target_pairs={{0,2},{1,3},{2,0},{3,1},{4,6},{5,7},{6,4},{7,5},{8,10},{9,11},{10,... | collective-permute-start | bytes 2162696 | tf_op jit(solution)/shard_map/ppermute | solution.py:149
  417.1 40.5 %collective-permute-start.32 = (bf16[2,2,2,2,96,768]{5,4,3,2,1,0:T(8,128)(2,1)S(1)}, bf16[2,2,2,2,96,768]{5,4,3,2,1,0:T(8,128)(2,1)S(1)}, u32[]{:S(2)}, u32[]{:S(2)}) collective-permute-start(bf16[2,2,2,2,96,768]{5,4,3,2,1,0:T(8,128)(2,1)S(1)} %copy-done.26), channel_id=1, source_target_pairs={{0,1},{1,0},{2,3},{3,2},{4,5},{5,4},{6,7},{7,6},{8,9},{9,8},{10,11... | collective-permute-start | bytes 7077896 | tf_op jit(solution)/shard_map/ppermute | solution.py:149
  420.6 50.1 %collective-permute-start.48 = (bf16[2,2,2,128,512]{4,3,1,0,2:T(8,128)(2,1)S(1)}, bf16[2,2,2,128,512]{4,3,1,0,2:T(8,128)(2,1)S(1)}, u32[]{:S(2)}, u32[]{:S(2)}) collective-permute-start(bf16[2,2,2,128,512]{4,3,1,0,2:T(8,128)(2,1)S(1)} %dynamic-slice_bitcast_fusion.5), channel_id=1, source_target_pairs={{0,16},{16,0},{1,17},{17,1},{2,18},{18,2},{3,19},{19,3},{4,20},{20... | collective-permute-start | bytes 3145736 | tf_op jit(solution)/shard_map/ppermute | solution.py:149
  431.6 22.8 %collective-permute-start.44 = (bf16[2,2,88,512]{3,2,1,0:T(8,128)(2,1)S(1)}, bf16[2,2,88,512]{3,2,1,0:T(8,128)(2,1)S(1)}, u32[]{:S(2)}, u32[]{:S(2)}) collective-permute-start(bf16[2,2,88,512]{3,2,1,0:T(8,128)(2,1)S(1)} %dynamic-slice_bitcast_fusion.11), channel_id=1, source_target_pairs={{0,16},{16,0},{1,17},{17,1},{2,18},{18,2},{3,19},{19,3},{4,20},{20... | collective-permute-start | bytes 1081352 | tf_op jit(solution)/shard_map/ppermute | solution.py:149
  434.8 44.9 %collective-permute-start.28 = (bf16[2,2,2,96,768]{4,3,2,1,0:T(8,128)(2,1)S(1)}, bf16[2,2,2,96,768]{4,3,2,1,0:T(8,128)(2,1)S(1)}, u32[]{:S(2)}, u32[]{:S(2)}) collective-permute-start(bf16[2,2,2,96,768]{4,3,2,1,0:T(8,128)(2,1)S(1)} %dynamic-slice_bitcast_fusion.4), channel_id=1, source_target_pairs={{0,16},{16,0},{1,17},{17,1},{2,18},{18,2},{3,19},{19,3},{4,20},{20... | collective-permute-start | bytes 3538952 | tf_op jit(solution)/shard_map/ppermute | solution.py:149
  438.9 69.3 %collective-permute-start.38 = (bf16[2,2,2,96,768]{4,3,1,0,2:T(8,128)(2,1)S(1)}, bf16[2,2,2,96,768]{4,3,1,0,2:T(8,128)(2,1)S(1)}, u32[]{:S(2)}, u32[]{:S(2)}) collective-permute-start(bf16[2,2,2,96,768]{4,3,1,0,2:T(8,128)(2,1)S(1)} %dynamic-slice_bitcast_fusion.2), channel_id=1, source_target_pairs={{0,16},{16,0},{1,17},{17,1},{2,18},{18,2},{3,19},{19,3},{4,20},{20... | collective-permute-start | bytes 3538952 | tf_op jit(solution)/shard_map/ppermute | solution.py:149
  454.5 10.9 %collective-permute-start.45 = (bf16[2,88,512]{2,1,0:T(8,128)(2,1)S(1)}, bf16[2,88,512]{2,1,0:T(8,128)(2,1)S(1)}, u32[]{:S(2)}, u32[]{:S(2)}) collective-permute-start(bf16[2,88,512]{2,1,0:T(8,128)(2,1)S(1)} %dynamic-slice_bitcast_fusion.16), channel_id=1, source_target_pairs={{0,8},{1,9},{2,10},{3,11},{4,12},{5,13},{6,14},{7,15},{8,0},{9,1},... | collective-permute-start | bytes 540680 | tf_op jit(solution)/shard_map/ppermute | solution.py:149
  465.7 51.3 %collective-permute-start.33 = (bf16[2,2,2,96,768]{4,3,2,1,0:T(8,128)(2,1)S(1)}, bf16[2,2,2,96,768]{4,3,2,1,0:T(8,128)(2,1)S(1)}, u32[]{:S(2)}, u32[]{:S(2)}) collective-permute-start(bf16[2,2,2,96,768]{4,3,2,1,0:T(8,128)(2,1)S(1)} %dynamic-slice_bitcast_fusion.3), channel_id=1, source_target_pairs={{0,2},{1,3},{2,0},{3,1},{4,6},{5,7},{6,4},{7,5},{8,10},{9,11},{10,... | collective-permute-start | bytes 3538952 | tf_op jit(solution)/shard_map/ppermute | solution.py:149
  471.1 34.8 %collective-permute-start.49 = (bf16[2,2,128,512]{3,2,1,0:T(8,128)(2,1)S(1)}, bf16[2,2,128,512]{3,2,1,0:T(8,128)(2,1)S(1)}, u32[]{:S(2)}, u32[]{:S(2)}) collective-permute-start(bf16[2,2,128,512]{3,2,1,0:T(8,128)(2,1)S(1)} %dynamic-slice_bitcast_fusion.10), channel_id=1, source_target_pairs={{0,2},{1,3},{2,0},{3,1},{4,6},{5,7},{6,4},{7,5},{8,10},{9,11},{10,... | collective-permute-start | bytes 1572872 | tf_op jit(solution)/shard_map/ppermute | solution.py:149
  480.0 43.0 %collective-permute-start.29 = (bf16[2,2,96,768]{3,2,1,0:T(8,128)(2,1)S(1)}, bf16[2,2,96,768]{3,2,1,0:T(8,128)(2,1)S(1)}, u32[]{:S(2)}, u32[]{:S(2)}) collective-permute-start(bf16[2,2,96,768]{3,2,1,0:T(8,128)(2,1)S(1)} %dynamic-slice_bitcast_fusion.9), channel_id=1, source_target_pairs={{0,2},{1,3},{2,0},{3,1},{4,6},{5,7},{6,4},{7,5},{8,10},{9,11},{10,... | collective-permute-start | bytes 1769480 | tf_op jit(solution)/shard_map/ppermute | solution.py:149
  506.1 10.4 %collective-permute-start.50 = (bf16[2,128,512]{2,1,0:T(8,128)(2,1)S(1)}, bf16[2,128,512]{2,1,0:T(8,128)(2,1)S(1)}, u32[]{:S(2)}, u32[]{:S(2)}) collective-permute-start(bf16[2,128,512]{2,1,0:T(8,128)(2,1)S(1)} %dynamic-slice_bitcast_fusion.15), channel_id=1, source_target_pairs={{0,8},{1,9},{2,10},{3,11},{4,12},{5,13},{6,14},{7,15},{8,0},{9,1},... | collective-permute-start | bytes 786440 | tf_op jit(solution)/shard_map/ppermute | solution.py:149
  508.6 20.3 %collective-permute-start.39 = (bf16[2,2,96,768]{3,2,1,0:T(8,128)(2,1)S(1)}, bf16[2,2,96,768]{3,2,1,0:T(8,128)(2,1)S(1)}, u32[]{:S(2)}, u32[]{:S(2)}) collective-permute-start(bf16[2,2,96,768]{3,2,1,0:T(8,128)(2,1)S(1)} %dynamic-slice_bitcast_fusion.7), channel_id=1, source_target_pairs={{0,2},{1,3},{2,0},{3,1},{4,6},{5,7},{6,4},{7,5},{8,10},{9,11},{10,... | collective-permute-start | bytes 1769480 | tf_op jit(solution)/shard_map/ppermute | solution.py:149
  517.3 13.6 %collective-permute-start.34 = (bf16[2,2,96,768]{3,2,1,0:T(8,128)(2,1)S(1)}, bf16[2,2,96,768]{3,2,1,0:T(8,128)(2,1)S(1)}, u32[]{:S(2)}, u32[]{:S(2)}) collective-permute-start(bf16[2,2,96,768]{3,2,1,0:T(8,128)(2,1)S(1)} %dynamic-slice_bitcast_fusion.8), channel_id=1, source_target_pairs={{0,16},{16,0},{1,17},{17,1},{2,18},{18,2},{3,19},{19,3},{4,20},{20... | collective-permute-start | bytes 1769480 | tf_op jit(solution)/shard_map/ppermute | solution.py:149
  523.2 26.0 %collective-permute-start.30 = (bf16[2,96,768]{2,1,0:T(8,128)(2,1)S(1)}, bf16[2,96,768]{2,1,0:T(8,128)(2,1)S(1)}, u32[]{:S(2)}, u32[]{:S(2)}) collective-permute-start(bf16[2,96,768]{2,1,0:T(8,128)(2,1)S(1)} %dynamic-slice_bitcast_fusion.14), channel_id=1, source_target_pairs={{0,8},{1,9},{2,10},{3,11},{4,12},{5,13},{6,14},{7,15},{8,0},{9,1},... | collective-permute-start | bytes 884744 | tf_op jit(solution)/shard_map/ppermute | solution.py:149
  529.1 26.6 %collective-permute-start.40 = (bf16[2,96,768]{2,1,0:T(8,128)(2,1)S(1)}, bf16[2,96,768]{2,1,0:T(8,128)(2,1)S(1)}, u32[]{:S(2)}, u32[]{:S(2)}) collective-permute-start(bf16[2,96,768]{2,1,0:T(8,128)(2,1)S(1)} %dynamic-slice_bitcast_fusion.12), channel_id=1, source_target_pairs={{0,8},{1,9},{2,10},{3,11},{4,12},{5,13},{6,14},{7,15},{8,0},{9,1},... | collective-permute-start | bytes 884744 | tf_op jit(solution)/shard_map/ppermute | solution.py:149
  531.1 28.3 %collective-permute-start.35 = (bf16[2,96,768]{2,1,0:T(8,128)(2,1)S(1)}, bf16[2,96,768]{2,1,0:T(8,128)(2,1)S(1)}, u32[]{:S(2)}, u32[]{:S(2)}) collective-permute-start(bf16[2,96,768]{2,1,0:T(8,128)(2,1)S(1)} %dynamic-slice_bitcast_fusion.13), channel_id=1, source_target_pairs={{0,8},{1,9},{2,10},{3,11},{4,12},{5,13},{6,14},{7,15},{8,0},{9,1},... | collective-permute-start | bytes 884744 | tf_op jit(solution)/shard_map/ppermute | solution.py:149
  549.3 13.1 %collective-permute-start.31 = (bf16[96,768]{1,0:T(8,128)(2,1)S(1)}, bf16[96,768]{1,0:T(8,128)(2,1)S(1)}, u32[]{:S(2)}, u32[]{:S(2)}) collective-permute-start(bf16[96,768]{1,0:T(8,128)(2,1)S(1)} %dynamic-slice_bitcast_fusion.19), channel_id=1, source_target_pairs={{0,4},{1,5},{2,6},{3,7},{4,0},{5,1},{6,2},{7,3},{8,12},{9,13},{10,... | collective-permute-start | bytes 442376 | tf_op jit(solution)/shard_map/ppermute | solution.py:149
  555.7 13.0 %collective-permute-start.41 = (bf16[96,768]{1,0:T(8,128)(2,1)S(1)}, bf16[96,768]{1,0:T(8,128)(2,1)S(1)}, u32[]{:S(2)}, u32[]{:S(2)}) collective-permute-start(bf16[96,768]{1,0:T(8,128)(2,1)S(1)} %dynamic-slice_bitcast_fusion.17), channel_id=1, source_target_pairs={{0,4},{1,5},{2,6},{3,7},{4,0},{5,1},{6,2},{7,3},{8,12},{9,13},{10,... | collective-permute-start | bytes 442376 | tf_op jit(solution)/shard_map/ppermute | solution.py:149
  (108 other events, 895.1 us)
